TPU v7x, 256 devices: a whole 4x4x8 slice. The times are simulated.
256 devices in a mesh: dp: 32 (over y_hi, z, core), tensor: 8 (over y_lo, x).
Axes of the slice: x: 4, y: 4 (y_hi: 2, y_lo: 2; y = y_hi * 2 + y_lo), z: 8, core: 2. Of those that a mesh axis runs over, the one named last changes fastest.
Arguments:
- roll_x: bfloat16 [512, 8192], P('dp', 'tensor'), may hold values from -6 to 6
- queries: bfloat16 [512, 8192], P('dp', 'tensor'), may hold values from -128 to 128, as said below
- cache_k: bfloat16 [512, 256, 1024], P('dp', None, 'tensor'), may hold values from -4 to 4
- cache_v: bfloat16 [512, 256, 1024], P('dp', None, 'tensor'), may hold values from -6 to 6
- cache_len: int32 [512], P('dp'), may hold values from 2 to 256
- tenant_roll: int32 [512], P('dp'), may hold values from 0 to 63
- w_key: bfloat16 [8192, 1024], P(None, 'tensor'), may hold values from -0.0625 to 0.0625
- w_value: bfloat16 [8192, 1024], P(None, 'tensor'), may hold values from -0.0625 to 0.0625
- ia3_key: float32 [64, 1024], replicated, may hold values from 0.25 to 1.75
- ia3_value: float32 [64, 1024], replicated, may hold values from 0.25 to 1.75
- train_x: bfloat16 [65536, 8192], P(('dp', 'tensor')), may hold values from -6 to 6
- upstream: bfloat16 [65536, 1024], P(('dp', 'tensor')), may hold values from -24 to 24
- tenant_train: int32 [65536], P(('dp', 'tensor')), may hold values from 0 to 63, as said below
- advantage: int32 [65536], P(('dp', 'tensor')), may hold values from -3 to 3
Outputs:
- attn_out: bfloat16 [512, 8192], P('dp', 'tensor')
- grad_ia3_value: float32 [64, 1024], P('dp', 'tensor')
- tenant_loss: float32 [64], replicated
Inputs may be any that keep to these rules, and one draw needn't show every extreme that they name: `queries`: query entries lie within the stated range. `tenant_train`: some tenants have no scored tokens.
All inputs are finite; a program needn't handle non-finite values.
Results may differ from a plain program's by a relative error of at most 0.0055.
Values may be sent and summed in bfloat16 or wider, within the bound.
A program may use at most 128 MiB of HBM per device.

v0:
```python
import functools

import jax
import jax.numpy as jnp
from jax import lax
from jax.sharding import Mesh
from jax.sharding import PartitionSpec as P

HD = 128
TENANTS = 64
DP = ("dp_0", "dp_1", "dp_2")
TENSOR = ("tensor_0", "tensor_1")
DP_TENSOR = ("dp_0", "dp_1", "dp_2", "tensor_0", "tensor_1")


def rows_first(arrays, axis, dims):
    turned = [jnp.moveaxis(a, dim, 0) for a, dim in zip(arrays, dims)]
    widths = [t[0].size for t in turned]
    both = jnp.concatenate([t.reshape(-1, w) for t, w in zip(turned, widths)], axis=1)
    result = lax.all_gather(both, axis, axis=0, tiled=True)
    pieces = jnp.split(result, [sum(widths[:k]) for k in range(1, len(widths))], axis=1)
    return tuple(
        (
            jnp.moveaxis(b.reshape(-1, *t.shape[1:]), 0, dim)
            for b, t, dim in zip(pieces, turned, dims)
        )
    )


def in_blocks(shard, dim, size):
    before, after = (shard.shape[:dim], shard.shape[dim + 1 :])
    return jnp.moveaxis(shard.reshape(*before, size, -1, *after), dim, 0)


def summed_on_arrival(shard, axis, dim):
    pieces = in_blocks(shard, dim, lax.axis_size(axis))
    arrived = lax.all_to_all(pieces, axis, split_axis=0, concat_axis=0, tiled=True)
    return arrived.sum(axis=0)


def by_axis(shard, axes):
    return functools.reduce(lax.psum, axes, shard)


def tenant_table(tenant):
    return (tenant[:, None] == jnp.arange(TENANTS, dtype=jnp.int32)[None, :]).astype(jnp.float32)


def local(
    roll_x,
    queries,
    cache_k,
    cache_v,
    cache_len,
    tenant_roll,
    w_key,
    w_value,
    ia3_key,
    ia3_value,
    train_x,
    upstream,
    tenant_train,
    advantage,
):
    high = lax.Precision.HIGHEST
    row_count = roll_x.shape[0]
    local_width = w_key.shape[1]
    heads_local = local_width // HD
    group_size = queries.shape[1] // local_width
    cache_size = cache_k.shape[1]
    dp_count = lax.axis_size(DP)
    column = lax.axis_index(TENSOR) * local_width
    fragment = lax.all_gather(roll_x, TENSOR, axis=1, tiled=True)
    key_sum = jnp.dot(fragment, w_key, preferred_element_type=jnp.float32)
    value_sum = jnp.dot(fragment, w_value, preferred_element_type=jnp.float32)
    onehot_roll = tenant_table(tenant_roll)
    key_gain = jnp.dot(
        onehot_roll, lax.dynamic_slice_in_dim(ia3_key, column, local_width, 1), precision=high
    )
    value_gain = jnp.dot(
        onehot_roll, lax.dynamic_slice_in_dim(ia3_value, column, local_width, 1), precision=high
    )
    key_new = (key_sum * key_gain).astype(jnp.bfloat16)
    value_new = (value_sum * value_gain).astype(jnp.bfloat16)
    scale_factor = 1.0 / jnp.sqrt(jnp.float32(HD))
    query_heads = queries.reshape(row_count, heads_local, group_size, HD)
    key_cache = cache_k.reshape(row_count, cache_size, heads_local, HD)
    value_cache = cache_v.reshape(row_count, cache_size, heads_local, HD)
    scores = (
        jnp.einsum("rkgd,rckd->rkgc", query_heads, key_cache, preferred_element_type=jnp.float32)
        * scale_factor
    )
    new_score = (
        jnp.einsum(
            "rkgd,rkd->rkg",
            query_heads,
            key_new.reshape(row_count, heads_local, HD),
            preferred_element_type=jnp.float32,
        )
        * scale_factor
    )
    in_cache = (jnp.arange(cache_size, dtype=jnp.int32)[None, :] < cache_len[:, None])[
        :, None, None, :
    ]
    scores = jnp.where(in_cache, scores, -jnp.inf)
    highest = jnp.maximum(jnp.max(scores, axis=-1), new_score)
    expo = jnp.exp(scores - highest[..., None])
    expo_new = jnp.exp(new_score - highest)
    denominator = jnp.sum(expo, axis=-1) + expo_new
    weights = (expo / denominator[..., None]).astype(jnp.bfloat16)
    weight_new = (expo_new / denominator).astype(jnp.bfloat16)
    mixed = jnp.einsum("rkgc,rckd->rkgd", weights, value_cache, preferred_element_type=jnp.float32)
    mixed = mixed + weight_new.astype(jnp.float32)[..., None] * value_new.astype(
        jnp.float32
    ).reshape(row_count, heads_local, 1, HD)
    attn_out = mixed.reshape(row_count, heads_local * group_size * HD).astype(jnp.bfloat16)
    onehot_own = tenant_table(tenant_train)
    values = jnp.dot(
        lax.all_gather(train_x, TENSOR, axis=0, tiled=True),
        w_value,
        preferred_element_type=jnp.float32,
    )
    labels, advantages = rows_first((tenant_train, advantage), TENSOR, (0, 0))
    cotangent = lax.all_to_all(upstream, TENSOR, split_axis=1, concat_axis=0, tiled=True).astype(
        jnp.float32
    )
    onehot_group = tenant_table(labels)
    gain_rows = jnp.dot(
        onehot_group, lax.dynamic_slice_in_dim(ia3_value, column, local_width, 1), precision=high
    )
    weighted = advantages.astype(jnp.float32)[:, None] * cotangent * values
    grad_block = summed_on_arrival(jnp.dot(onehot_group.T, weighted, precision=high), DP, 0)
    loss_part = jnp.dot(onehot_group.T, jnp.sum(weighted * gain_rows, axis=1), precision=high)
    counts, loss_total = (
        by_axis(jnp.sum(onehot_own, axis=0), DP_TENSOR),
        by_axis(loss_part, DP_TENSOR),
    )
    divisor = jnp.maximum(counts, 1.0)
    per_index = TENANTS // dp_count
    own_divisor = lax.dynamic_slice_in_dim(divisor, lax.axis_index(DP) * per_index, per_index, 0)
    gradient = -grad_block / own_divisor[:, None]
    tenant_loss = -loss_total / divisor
    return (attn_out, gradient, tenant_loss)


def solution(mesh):
    finer = Mesh(
        mesh.devices.reshape(2, 8, 2, 2, 4), ("dp_0", "dp_1", "dp_2", "tensor_0", "tensor_1")
    )
    placed = (
        P(DP, TENSOR),
        P(DP, TENSOR),
        P(DP, None, TENSOR),
        P(DP, None, TENSOR),
        P(DP),
        P(DP),
        P(None, TENSOR),
        P(None, TENSOR),
        P(),
        P(),
        P(DP_TENSOR, None),
        P(DP_TENSOR, None),
        P(DP_TENSOR),
        P(DP_TENSOR),
    )
    return jax.shard_map(
        local,
        mesh=finer,
        in_specs=placed,
        out_specs=(P(DP, TENSOR), P(DP, TENSOR), P()),
        check_vma=False,
    )
```

profile of v0, /device:TPU:1, one launch (start us, length us, event | category | flops | bytes accessed | tf_op | source)
XLA Modules:
  0.0 419.7 jit_solution(4356088209422669333)
XLA Ops:
  7.2 0.0 copy-start
  7.2 0.0 copy-start.2
  7.2 0.0 all-gather.2.cloned.1.call-start
  7.2 0.7 all-gather.2.cloned.1.call-update
  7.9 0.4 copy-done.2
  8.4 1.0 copy.21
  9.4 6.0 %all-to-all-start = ((bf16[256,8,128]{0,2,1:T(8,128)(2,1)}), bf16[256,8,128]{0,2,1:T(8,128)(2,1)S(1)}, u32[]{:S(2)}, u32[]{:S(2)}) async-start(bf16[256,8,128]{0,2,1:T(8,128)(2,1)} %bitcast.7), calls=%async_computation | async-start | bytes 1048576 | tf_op jit(solution)/shard_map/all_to_all | solution.py:124
  15.4 0.0 copy-done.4
  15.4 0.0 copy-done.6
  15.4 0.0 copy-start.1
  15.4 0.1 convert_reduce_fusion
  15.5 0.0 copy-done.3
  15.5 29.9 %all_gather.9 = bf16[16,8192]{1,0:T(8,128)(2,1)S(1)} all-gather(bf16[16,1024]{1,0:T(8,128)(2,1)S(1)} %copy-done.3), channel_id=1, replica_groups=mesh['dp_0'=2,'dp_1'=8,'dp_2'=2,'tensor_0'=2,'tensor_1'=4] {'tensor_0','..., dimensions={1}, use_global_device_ids=true | all-gather | bytes 294912 | tf_op jit(solution)/shard_map/all_gather | solution.py:73
  45.4 2.0 fusion.30
  47.4 0.0 copy-done.9
  47.5 0.0 copy-start.8
  47.5 1.0 fusion.6
  48.5 0.0 copy-done.7
  48.5 0.1 iota_compare_fusion.5
  48.6 0.1 fusion.19
  48.7 0.0 copy-done.1
  48.7 0.5 fusion.29
  49.2 0.2 fusion.13
  49.4 0.0 copy-done
  49.4 0.4 fusion.31
  49.8 0.9 fusion.5
  50.8 0.3 fusion.2
  51.1 0.0 copy-done.5
  51.1 0.6 copy.31
  51.7 21.6 %all_gather.10 = s32[2048,2]{0,1:T(2,128)S(1)} all-gather(s32[256,2]{0,1:T(2,128)S(1)} %pad_add_fusion), channel_id=1, replica_groups=mesh['dp_0'=2,'dp_1'=8,'dp_2'=2,'tensor_0'=2,'tensor_1'=4] {'tensor_0','..., dimensions={0}, use_global_device_ids=true | all-gather | bytes 18432 | tf_op jit(solution)/shard_map/all_gather | solution.py:20
  73.4 0.0 all-to-all-done
  73.4 0.1 convert_bitcast_fusion
  73.5 0.1 copy.25
  73.6 272.8 %all-gather.2.cloned.1.call-done = bf16[2048,8192]{1,0:T(8,128)(2,1)} async-done(((bf16[256,8192]{1,0:T(8,128)(2,1)}), bf16[2048,8192]{1,0:T(8,128)(2,1)}) %all-gather.2.cloned.1.call-update) | async-done | bytes 33554448 | tf_op jit(solution)/shard_map/all_gather | solution.py:119
  346.4 15.6 %convolution_multiply_fusion.1 = f32[2048,128]{0,1:T(8,128)S(1)} fusion(bf16[2048,8192]{1,0:T(8,128)(2,1)} %all-gather.2.cloned.1.call-done, bf16[8192,128]{1,0:T(8,128)(2,1)S(1)} %copy-done, f32[2048,128]{0,1:T(8,128)S(1)} %bitcast.35, f32[2048]{0:T(1024)S(1)} %bitcast.36), kind=kOutput, calls=%fused_computation.1 | convolution fusion | flops 4295491584 | bytes 37756928 | tf_op jit(solution)/shard_map/dot_general | solution.py:118
  362.0 1.7 fusion
  363.7 1.8 fusion.8
  365.5 0.3 convolution_bitcast_fusion
  365.8 9.8 %all-to-all-start.1 = ((f32[32,2,128]{2,1,0:T(2,128)}), f32[32,2,128]{2,1,0:T(2,128)S(1)}, u32[]{:S(2)}, u32[]{:S(2)}) async-start(f32[32,2,128]{2,1,0:T(2,128)} %bitcast.9), calls=%async_computation.1 | async-start | bytes 65536 | tf_op jit(solution)/shard_map/all_to_all | solution.py:37
  375.7 5.6 %all-reduce.4 = (f32[64]{0:T(128)S(1)}, f32[64]{0:T(128)S(1)}) all-reduce(f32[64]{0:T(128)S(1)} %convert_reduce_fusion, f32[64]{0:T(128)S(1)} %convolution_bitcast_fusion), channel_id=1, replica_groups=mesh['dp_0'=2,'dp_1'=8,'dp_2'=2,'tensor_0'=2,'tensor_1'=4] {'dp_0'}, use_global_device_ids=true, to_apply=%region_4.5 | all-reduce | flops 128 | bytes 1024 | tf_op jit(solution)/shard_map/psum | solution.py:42
  381.3 13.3 %all-reduce = (f32[64]{0:T(128)S(1)}, f32[64]{0:T(128)S(1)}) all-reduce(f32[64]{0:T(128)S(1)} %get-tuple-element.11, f32[64]{0:T(128)S(1)} %get-tuple-element.12), channel_id=1, replica_groups=mesh['dp_0'=2,'dp_1'=8,'dp_2'=2,'tensor_0'=2,'tensor_1'=4] {'dp_1'}, use_global_device_ids=true, to_apply=%region_5.6 | all-reduce | flops 128 | bytes 1024 | tf_op jit(solution)/shard_map/psum | solution.py:42
  394.5 7.1 %all-reduce.3 = (f32[64]{0:T(128)S(1)}, f32[64]{0:T(128)S(1)}) all-reduce(f32[64]{0:T(128)S(1)} %get-tuple-element.3, f32[64]{0:T(128)S(1)} %get-tuple-element.4), channel_id=1, replica_groups=mesh['dp_0'=2,'dp_1'=8,'dp_2'=2,'tensor_0'=2,'tensor_1'=4] {'dp_2'}, use_global_device_ids=true, to_apply=%region_6.7 | all-reduce | flops 128 | bytes 1024 | tf_op jit(solution)/shard_map/psum | solution.py:42
  401.6 3.8 all-reduce.2
  405.4 6.2 %all-reduce.1 = (f32[64]{0:T(128)S(1)}, f32[64]{0:T(128)S(1)}) all-reduce(f32[64]{0:T(128)S(1)} %get-tuple-element.7, f32[64]{0:T(128)S(1)} %get-tuple-element.8), channel_id=1, replica_groups=mesh['dp_0'=2,'dp_1'=8,'dp_2'=2,'tensor_0'=2,'tensor_1'=4] {'tensor_1'}, use_global_device_ids=true, to_apply=%region_8.9 | all-reduce | flops 128 | bytes 1024 | tf_op jit(solution)/shard_map/psum | solution.py:42
  411.6 0.5 negate_divide_fusion.1
  412.1 0.1 dynamic_slice.12
  412.2 0.0 all-to-all-done.1
  412.2 0.6 negate_divide_fusion
  (13 shorter events, 0.1 us)
Async XLA Ops:
  7.2 42.2 %copy-start = (bf16[8192,128]{1,0:T(8,128)(2,1)S(1)}, bf16[8192,128]{1,0:T(8,128)(2,1)}, u32[]{:S(2)}) copy-start(bf16[8192,128]{1,0:T(8,128)(2,1)} %param.21) | copy-start | bytes 6291460
  7.2 1.2 copy-start.2
  7.2 339.2 %all-gather.2.cloned.1.call-start = ((), (), s32[]{:S(2)}) async-start(), calls=%async_computation.2 | async-start | bytes 37748736 | tf_op jit(solution)/shard_map/all_gather | solution.py:119
  8.4 7.0 %copy-start.4 = (bf16[16,1024]{1,0:T(8,128)(2,1)S(1)}, bf16[16,1024]{1,0:T(8,128)(2,1)}, u32[]{:S(2)}) copy-start(bf16[16,1024]{1,0:T(8,128)(2,1)} %param.15) | copy-start | bytes 98308
  8.4 7.0 %copy-start.6 = (s32[256]{0:T(256)S(1)}, s32[256]{0:T(256)}, u32[]{:S(2)}) copy-start(s32[256]{0:T(256)} %param.26) | copy-start | bytes 3076
  8.4 7.2 %copy-start.3 = (bf16[16,1024]{1,0:T(8,128)(2,1)S(1)}, bf16[16,1024]{1,0:T(8,128)(2,1)}, u32[]{:S(2)}) copy-start(bf16[16,1024]{1,0:T(8,128)(2,1)} %param.14) | copy-start | bytes 98308
  9.4 38.1 %copy-start.9 = (s32[16]{0:T(128)S(1)}, s32[16]{0:T(128)}, u32[]{:S(2)}) copy-start(s32[16]{0:T(128)} %param.19) | copy-start | bytes 196
  9.4 39.1 %copy-start.7 = (s32[16]{0:T(128)S(1)}, s32[16]{0:T(128)}, u32[]{:S(2)}) copy-start(s32[16]{0:T(128)} %param.18) | copy-start | bytes 196
  9.4 64.0 %all-to-all-start = ((bf16[256,8,128]{0,2,1:T(8,128)(2,1)}), bf16[256,8,128]{0,2,1:T(8,128)(2,1)S(1)}, u32[]{:S(2)}, u32[]{:S(2)}) async-start(bf16[256,8,128]{0,2,1:T(8,128)(2,1)} %bitcast.7), calls=%async_computation | async-start | bytes 1048576 | tf_op jit(solution)/shard_map/all_to_all | solution.py:124
  15.4 33.3 %copy-start.1 = (bf16[16,256,128]{2,1,0:T(8,128)(2,1)S(1)}, bf16[16,256,128]{2,1,0:T(8,128)(2,1)}, u32[]{:S(2)}) copy-start(bf16[16,256,128]{2,1,0:T(8,128)(2,1)} %param.16) | copy-start | bytes 3145732
  47.5 3.3 copy-start.8
  49.2 1.9 copy-start.5
  365.8 46.3 %all-to-all-start.1 = ((f32[32,2,128]{2,1,0:T(2,128)}), f32[32,2,128]{2,1,0:T(2,128)S(1)}, u32[]{:S(2)}, u32[]{:S(2)}) async-start(f32[32,2,128]{2,1,0:T(2,128)} %bitcast.9), calls=%async_computation.1 | async-start | bytes 65536 | tf_op jit(solution)/shard_map/all_to_all | solution.py:37
Sparse Core Ops, SparseCore 0:
  9.8 336.5 all-gather.1
where the time goes:
time: 422 us; the launch traced here: 420 us
  waiting for transfers between devices  273 us (65%)
  blocking collectives  87.4 us (21%)
  matrix products  24.7 us (6%)
  starting transfers between devices  15.9 us (4%)
  between operations  14.2 us (3%)
    all_gather x1, waiting for transfers between devices, local(): lax.all_gather(train_x, TENSOR, axis=0, tiled=True)  273 us
    psum x5, blocking collectives, by_axis(): return functools.reduce(lax.psum, axes, shard)  35.9 us
    all_gather x1, blocking collectives, local(): fragment = lax.all_gather(roll_x, TENSOR, axis=1, tiled=True)  29.9 us
    all_gather x1, blocking collectives, rows_first(): result = lax.all_gather(both, axis, axis=0, tiled=True)  21.6 us
    dot_general x1, matrix products, local(): jnp.dot(lax.all_gather(train_x, TENSOR, axis=0, tiled=True), w_value, pre...  15.6 us
    all_to_all x1, starting transfers between devices, summed_on_arrival(): lax.all_to_all(pieces, axis, split_axis=0, concat_axis=0, tiled=True)  9.83 us
  transfers between devices with their start and end apart: 3, of which 1 were waited for; matrix products, arithmetic and copies ran while one was open for 2% of the time, Pallas kernels for 0%

commit v1 on v0

v1 whole, which is shorter than its diff:
```python
import jax
import jax.numpy as jnp
from jax import lax
from jax.experimental import pallas as pl
from jax.experimental.pallas import tpu as pltpu
from jax.sharding import Mesh
from jax.sharding import PartitionSpec as P

HD = 128
TENANTS = 64
AXES = ("y_hi", "z", "core", "y_lo", "x")
DP = ("y_hi", "z", "core")
TENSOR = ("y_lo", "x")
DP_TENSOR = DP + TENSOR
MESH = pl.DeviceIdType.MESH
F32 = jnp.float32
BF16 = jnp.bfloat16

O, XM, XP, X2, F0, FM, FP, F2 = range(8)
SHIFT = ((0, 0), (0, 3), (0, 1), (0, 2), (1, 0), (1, 3), (1, 1), (1, 2))
INVERSE = (O, XP, XM, X2, F0, FP, FM, F2)

HALF = 4096
ZROWS = 1024
QROWS = (HALF - ZROWS) // 4
ZHALF = ZROWS // 2

FROM_XM = ((XM, 0), (XM, 1), (XM, 2), (X2, 0), (X2, 2), (XM, 3), (FM, 3))
FROM_XP = ((XP, 0), (XP, 1), (XP, 3), (X2, 1), (X2, 3), (XP, 2), (FP, 2))
FROM_YM = ((F0, 0), (F0, 2), (FM, 0), (FM, 1), (FM, 2), (F2, 0), (F2, 2))
FROM_YP = ((F0, 1), (F0, 3), (FP, 0), (FP, 1), (FP, 3), (F2, 1), (F2, 3))
LINKS = (FROM_XM, FROM_XP, FROM_YM, FROM_YP)
SENT_AS = (
    {XM: O, X2: XM, FM: F0},
    {XP: O, X2: XP, FP: F0},
    {F0: O, FM: XM, FP: XP, F2: X2},
    {F0: O, FM: XM, FP: XP, F2: X2},
)
Z_SEND = {0: (F0,), 1: (XM, XP), 3: (X2, FM, FP), 5: (F2,)}
Z_TAKE = {2: (F0,), 3: (XM,), 4: (XP,), 5: (X2,), 6: (FM, FP, F2)}
COMPLETE = {2: (F0,), 5: (XM, XP, X2), 6: (FM, FP, F2)}


def dot(a, b):
    return jnp.dot(a, b, preferred_element_type=F32)


def exact_dot(a, b, dims):
    return lax.dot_general(
        a, b, (dims, ((), ())), precision=lax.Precision.HIGHEST, preferred_element_type=F32
    )


def kernel(
    clen, troll, roll_h, q_h, ck_h, cv_h, wk_h, wv_h, ik_h, iv_h, x_h, up_h, tt_h, adv_h,
    attn_o, grad_o, loss_o,
    wbuf, wv, wk, xh, up, kc, vc, q, rx, ik, iv, tt, adv, acc, pbuf, sbuf, gbuf, lmine, lbuf,
    msg, rbuf, qs, sc, mix, snew, mt, lacc, cnt,
    lsem, wsend, wrecv, zrecv, xsend, xrecv, rsend, rrecv, psend, precv, gsend, grecv,
    lsend, lrecv, msend, mrecv,
):
    y_hi, z, core, y_lo, x = (lax.axis_index(a) for a in AXES)
    d = y_hi * 16 + z * 2 + core
    t = y_lo * 4 + x
    odd = z % 2
    y = 2 * y_hi + y_lo
    y_up, y_down = (y + 1) % 4, (y + 3) % 4
    me = (y_hi, z, core, y_lo, x)
    sibling = (y_hi, z, 1 - core, y_lo, x)
    z_up = (y_hi, (z + 1) % 8, core, y_lo, x)
    z_down = (y_hi, (z + 7) % 8, core, y_lo, x)
    to_link = (
        (y_hi, z, core, y_lo, (x + 1) % 4),
        (y_hi, z, core, y_lo, (x + 3) % 4),
        (y_up // 2, z, core, y_up % 2, x),
        (y_down // 2, z, core, y_down % 2, x),
    )

    def place(block):
        return (y_lo + SHIFT[block][0]) % 2, (x + SHIFT[block][1]) % 4

    def peer(block):
        py, px = place(block)
        return (y_hi, z, core, py, px)

    def columns(block):
        py, px = place(block)
        return pl.ds(pl.multiple_of((py * 4 + px) * HD, HD), HD)

    def dp_peer(step):
        other = (d + step) % 32
        return other, (other // 16, (other // 2) % 8, other % 2, y_lo, x)

    def remote(src, dst, send, recv, device):
        return pltpu.make_async_remote_copy(
            src_ref=src, dst_ref=dst, send_sem=send, recv_sem=recv,
            device_id=device, device_id_type=MESH,
        )

    own_half = pl.ds(pl.multiple_of(core * HALF, HALF), HALF)
    other_half = pl.ds(pl.multiple_of((1 - core) * HALF, HALF), HALF)
    local = [
        pltpu.make_async_copy(src, dst, lsem.at[k])
        for k, (src, dst) in enumerate(
            (
                (wv_h, wv),
                (x_h.at[:, own_half], xh.at[pl.ds(0, 256)]),
                (tt_h, tt),
                (adv_h, adv),
                (up_h, up),
                (wk_h, wk),
                (roll_h, rx.at[t]),
                (ik_h.at[:, pl.ds(pl.multiple_of(t * HD, HD), HD)], ik),
                (iv_h, iv),
                (q_h, q),
                (ck_h, kc),
                (cv_h, vc),
            )
        )
    ]
    for copy in local:
        copy.start()

    barrier = pltpu.get_barrier_semaphore()

    def greet(step, carry):
        pl.semaphore_signal(barrier, inc=1, device_id=dp_peer(step)[1], device_id_type=MESH)
        return carry

    for block in range(1, 8):
        pl.semaphore_signal(barrier, inc=1, device_id=peer(block), device_id_type=MESH)
    pl.semaphore_signal(
        barrier, inc=1, device_id=(1 - y_hi, z, core, 1 - y_lo, x), device_id_type=MESH
    )
    lax.fori_loop(1, 32, greet, 0)
    pl.semaphore_wait(barrier, 39)

    def quarter(k):
        return pl.multiple_of(
            (1 - odd) * (k * QROWS) + odd * (HALF - (k + 1) * QROWS), 64
        )

    def link_copy(link, r):
        block, k = LINKS[link][r]
        source = SENT_AS[link][block]
        row = quarter(k)
        if source == O:
            src = wv_h.at[pl.ds(pl.multiple_of(core * HALF + row, 64), QROWS)]
        else:
            src = wbuf.at[source - 1, pl.ds(row, QROWS)]
        return remote(
            src, wbuf.at[block - 1, pl.ds(row, QROWS)], wsend, wrecv.at[link, r], to_link[link]
        )

    def z_copy(block, h, base):
        rows = pl.ds(pl.multiple_of(base + h * ZHALF, 64), ZHALF)
        ref = wbuf.at[block - 1, rows]
        return remote(ref, ref, wsend, zrecv.at[h, block - 1], z_up if h == 0 else z_down)

    z_sent = odd * (HALF - ZROWS)
    z_taken = (1 - odd) * (HALF - ZROWS)

    def issue(r):
        for link in range(4):
            link_copy(link, r).start()

    roll_sends = [
        remote(roll_h, rx.at[t], rsend, rrecv, peer(block)) for block in range(1, 8)
    ]
    x_copy = remote(x_h.at[:, other_half], xh.at[pl.ds(256, 256)], xsend, xrecv, sibling)
    issue(0)
    x_copy.start()
    for copy in roll_sends:
        copy.start()
    issue(1)

    def product(block, row, length, first=False):
        if block == O:
            part = wv[pl.ds(pl.multiple_of(core * HALF + row, 64), length), :]
        else:
            part = wbuf[block - 1, pl.ds(row, length), :]
        new = dot(xh[:, pl.ds(pl.multiple_of(row, 64), length)], part)
        if first:
            acc[block] = new
        else:
            acc[block] += new

    def partial_copy(block):
        return remote(
            acc.at[block, pl.ds(256, 256)], pbuf.at[block], psend, precv.at[block], sibling
        )

    def sum_copy(block):
        return remote(
            sbuf.at[block], gbuf.at[INVERSE[block] - 1], gsend, grecv, peer(block)
        )

    def finish(block, first=False):
        partial_copy(block).wait_recv()
        values = acc[block, 0:256, :] + pbuf[block]
        weighted = values * up[:, columns(block)].astype(F32)
        high = weighted.astype(BF16)
        low = (weighted - high.astype(F32)).astype(BF16)
        sums = dot(mt[...], high) + dot(mt[...], low)
        sbuf[block] = sums
        if block != O:
            sum_copy(block).start()
        part = sums * iv[:, columns(block)]
        if first:
            lacc[0:64, :] = part
        else:
            lacc[0:64, :] += part

    for k in (2, 3):
        local[k].wait()
    tenant = lax.broadcasted_iota(jnp.int32, (64, 128), 0)
    hits = [
        (tenant == jnp.broadcast_to(tt[k : k + 1, :], (64, 128))).astype(F32) for k in range(2)
    ]
    for k in range(2):
        gain = jnp.broadcast_to(adv[k : k + 1, :].astype(F32), (64, 128))
        mt[:, k * 128 : (k + 1) * 128] = (hits[k] * gain).astype(BF16)
    cnt[0:64, :] = hits[0] + hits[1]
    cnt[64:128, :] = jnp.zeros((64, 128), F32)
    lacc[64:128, :] = jnp.zeros((64, 128), F32)

    scale = 1.0 / jnp.sqrt(F32(HD))

    def spread(h, transposed=False):
        shape = (16, 128) if transposed else (128, 16)
        pair = lax.broadcasted_iota(jnp.int32, shape, 1 if transposed else 0)
        row = lax.broadcasted_iota(jnp.int32, shape, 0 if transposed else 1)
        if h is None:
            return (pair // 8 == row).astype(F32).astype(BF16)
        return (pair == row * 8 + h).astype(F32).astype(BF16)

    def project():
        for k in (5, 6, 7, 8, 9):
            local[k].wait()
        remote(rx.at[pl.ds(0, 7)], rx.at[pl.ds(0, 7)], rsend, rrecv, sibling).wait_recv()
        key_sum = jnp.zeros((16, HD), F32)
        value_sum = jnp.zeros((16, HD), F32)
        for k in range(8):
            part = rx[k]
            key_sum = key_sum + dot(part, wk[k * 1024 : (k + 1) * 1024, :])
            value_sum = value_sum + dot(part, wv[k * 1024 : (k + 1) * 1024, :])
        row = lax.broadcasted_iota(jnp.int32, (16, TENANTS), 0)
        owner = jnp.zeros((16, TENANTS), jnp.int32)
        for r in range(16):
            owner = jnp.where(row == r, troll[r], owner)
        onehot = (owner == lax.broadcasted_iota(jnp.int32, (16, TENANTS), 1)).astype(F32)
        key_gain = exact_dot(onehot, ik[...], ((1,), (0,)))
        value_gain = exact_dot(onehot, iv[:, columns(O)], ((1,), (0,)))
        key_new = (key_sum * key_gain).astype(BF16)
        value_new = (value_sum * value_gain).astype(BF16)
        queries = jnp.zeros((128, HD), F32)
        for h in range(8):
            queries = queries + dot(spread(h), q[:, h * HD : (h + 1) * HD])
        qs[...] = queries
        each = spread(None)
        snew[...] = jnp.broadcast_to(
            jnp.sum(queries * dot(each, key_new), axis=1, keepdims=True) * scale, (128, 128)
        )
        mix[...] = dot(each, value_new)

    def score():
        local[10].wait()
        place_in_cache = lax.broadcasted_iota(jnp.int32, (8, 256), 1)
        for r in range(16):
            s = lax.dot_general(
                qs[r * 8 : (r + 1) * 8, :].astype(BF16), kc[r], (((1,), (1,)), ((), ())),
                preferred_element_type=F32,
            ) * scale
            sc[r * 8 : (r + 1) * 8, :] = jnp.where(place_in_cache < clen[r], s, -jnp.inf)

    def normalise():
        s = sc[...]
        new = snew[:, 0:1]
        highest = jnp.maximum(jnp.max(s, axis=1, keepdims=True), new)
        expo = jnp.exp(s - highest)
        expo_new = jnp.exp(new - highest)
        denominator = jnp.sum(expo, axis=1, keepdims=True) + expo_new
        sc[...] = (expo / denominator).astype(BF16).astype(F32)
        mix[...] = (expo_new / denominator).astype(BF16).astype(F32) * mix[...]

    def mixture():
        local[11].wait()
        for r in range(16):
            rows = slice(r * 8, (r + 1) * 8)
            mix[rows, :] += dot(sc[rows, :].astype(BF16), vc[r])
        mixed = mix[...].astype(BF16)
        for h in range(8):
            attn_o[:, h * HD : (h + 1) * HD] = dot(spread(h, True), mixed).astype(BF16)

    beside = {0: project, 1: score, 2: normalise, 3: mixture}

    for k in (0, 1, 4):
        local[k].wait()
    x_copy.wait_recv()
    for k in range(4):
        product(O, k * 1024, 1024, k == 0)
    partial_copy(O).start()

    seen = {O}
    for r in range(7):
        for link in range(4):
            link_copy(link, r).wait_recv()
        if r + 2 < 7:
            issue(r + 2)
        for block in Z_SEND.get(r, ()):
            for h in range(2):
                z_copy(block, h, z_sent).start()
        for link in range(4):
            block, k = LINKS[link][r]
            product(block, quarter(k), QROWS, block not in seen)
            seen.add(block)
        for block in Z_TAKE.get(r, ()):
            for h in range(2):
                z_copy(block, h, z_taken).wait_recv()
            product(block, pl.multiple_of(z_taken, 64), ZROWS)
        for block in COMPLETE.get(r, ()):
            partial_copy(block).start()
        if r in beside:
            beside[r]()
        if r == 1:
            finish(O, True)
        if r == 3:
            finish(F0)
        if r == 5:
            for block in COMPLETE[5]:
                finish(block)
    for block in COMPLETE[6]:
        finish(block)

    ones = jnp.ones((8, 128), F32)
    tile_row = lax.broadcasted_iota(jnp.int32, (8, 128), 0)
    loss_row = exact_dot(ones, lacc[...], ((1,), (1,)))
    count_row = exact_dot(ones, cnt[...], ((1,), (1,)))
    mine = jnp.where(tile_row == 2, loss_row, jnp.where(tile_row == 3, count_row, 0.0))
    lmine[...] = mine
    for block in range(1, 8):
        remote(lmine, lbuf.at[t], lsend, lrecv, peer(block)).start()
    lbuf[t] = mine

    remote(gbuf, gbuf, gsend, grecv, sibling).wait_recv()
    total = sbuf[O]
    for k in range(7):
        total = total + gbuf[k]
    remote(lbuf.at[pl.ds(0, 7)], lbuf.at[pl.ds(0, 7)], lsend, lrecv, sibling).wait_recv()
    group = lbuf[0]
    for k in range(1, 8):
        group = group + lbuf[k]
    for k in range(32):
        msg[k] = group
        msg[k, 0:2, :] = total[2 * k : 2 * k + 2, :]

    def scatter(step, carry):
        other, device = dp_peer(step)
        remote(msg.at[other], rbuf.at[d], msend, mrecv, device).start()
        return carry

    lax.fori_loop(1, 32, scatter, 0)
    rbuf[d] = msg[d]
    remote(rbuf.at[pl.ds(0, 31)], rbuf.at[pl.ds(0, 31)], msend, mrecv, sibling).wait_recv()
    whole = rbuf[0]
    for k in range(1, 32):
        whole = whole + rbuf[k]
    divisor = jnp.maximum(whole[3:4, :], 1.0)
    loss_o[...] = -whole[2:3, :] / divisor
    lane = lax.broadcasted_iota(jnp.int32, (2, 128), 1)
    row = lax.broadcasted_iota(jnp.int32, (2, 128), 0)
    own = jnp.sum(
        jnp.where(lane == 2 * d + row, jnp.broadcast_to(divisor, (2, 128)), 0.0),
        axis=1, keepdims=True,
    )
    grad_o[...] = -whole[0:2, :] / own

    x_copy.wait_send()
    remote(rx.at[pl.ds(0, 7)], rx.at[pl.ds(0, 7)], rsend, rrecv, sibling).wait_send()
    remote(wbuf, wbuf, wsend, xrecv, sibling).wait_send()
    remote(pbuf, pbuf, psend, xrecv, sibling).wait_send()
    remote(gbuf, gbuf, gsend, grecv, sibling).wait_send()
    remote(lbuf.at[pl.ds(0, 7)], lbuf.at[pl.ds(0, 7)], lsend, lrecv, sibling).wait_send()
    remote(rbuf.at[pl.ds(0, 31)], rbuf.at[pl.ds(0, 31)], msend, mrecv, sibling).wait_send()


def local_step(
    roll_x, queries, cache_k, cache_v, cache_len, tenant_roll, w_key, w_value, ia3_key,
    ia3_value, train_x, upstream, tenant_train, advantage,
):
    smem = pl.BlockSpec(memory_space=pltpu.SMEM)
    vmem = pl.BlockSpec(memory_space=pltpu.VMEM)
    anywhere = pl.BlockSpec(memory_space=pl.ANY)
    dma = pltpu.SemaphoreType.DMA
    attn_out, gradient, tenant_loss = pl.pallas_call(
        kernel,
        out_shape=(
            jax.ShapeDtypeStruct((16, 1024), BF16),
            jax.ShapeDtypeStruct((2, 128), F32),
            jax.ShapeDtypeStruct((1, 128), F32),
        ),
        in_specs=[smem, smem] + [anywhere] * 12,
        out_specs=(vmem, vmem, vmem),
        scratch_shapes=[
            pltpu.VMEM((7, HALF, HD), BF16),
            pltpu.VMEM((2 * HALF, HD), BF16),
            pltpu.VMEM((2 * HALF, HD), BF16),
            pltpu.VMEM((512, HALF), BF16),
            pltpu.VMEM((256, 1024), BF16),
            pltpu.VMEM((16, 256, HD), BF16),
            pltpu.VMEM((16, 256, HD), BF16),
            pltpu.VMEM((16, 1024), BF16),
            pltpu.VMEM((8, 16, 1024), BF16),
            pltpu.VMEM((TENANTS, HD), F32),
            pltpu.VMEM((TENANTS, 1024), F32),
            pltpu.VMEM((2, 128), jnp.int32),
            pltpu.VMEM((2, 128), jnp.int32),
            pltpu.VMEM((8, 512, HD), F32),
            pltpu.VMEM((8, 256, HD), F32),
            pltpu.VMEM((8, TENANTS, HD), F32),
            pltpu.VMEM((7, TENANTS, HD), F32),
            pltpu.VMEM((8, 128), F32),
            pltpu.VMEM((8, 8, 128), F32),
            pltpu.VMEM((32, 8, 128), F32),
            pltpu.VMEM((32, 8, 128), F32),
            pltpu.VMEM((128, HD), F32),
            pltpu.VMEM((128, 256), F32),
            pltpu.VMEM((128, HD), F32),
            pltpu.VMEM((128, 128), F32),
            pltpu.VMEM((TENANTS, 256), BF16),
            pltpu.VMEM((128, 128), F32),
            pltpu.VMEM((128, 128), F32),
            dma((12,)), dma, dma((4, 7)), dma((2, 7)), dma, dma, dma, dma, dma, dma((8,)),
            dma, dma, dma, dma, dma, dma,
        ],
        compiler_params=pltpu.CompilerParams(
            collective_id=0, has_side_effects=True, vmem_limit_bytes=60 * 1024 * 1024
        ),
    )(
        cache_len, tenant_roll, roll_x, queries, cache_k, cache_v, w_key, w_value, ia3_key,
        ia3_value, train_x, upstream, tenant_train.reshape(2, 128), advantage.reshape(2, 128),
    )
    return attn_out, gradient, tenant_loss[0, :TENANTS]


def solution(mesh):
    finer = Mesh(mesh.devices.reshape(2, 8, 2, 2, 4), AXES)
    placed = (
        P(DP, TENSOR), P(DP, TENSOR), P(DP, None, TENSOR), P(DP, None, TENSOR), P(DP), P(DP),
        P(None, TENSOR), P(None, TENSOR), P(), P(), P(DP_TENSOR, None), P(DP_TENSOR, None),
        P(DP_TENSOR), P(DP_TENSOR),
    )
    return jax.shard_map(
        local_step, mesh=finer, in_specs=placed, out_specs=(P(DP, TENSOR), P(DP, TENSOR), P()),
        check_vma=False,
    )
```

time: 422 us -> 69.7 us (0.17)
  waiting for transfers between devices: 273 us -> 0 us
  blocking collectives: 87.4 us -> 0 us
  Pallas kernels: 0 us -> 65.2 us
  matrix products: 24.7 us -> 0 us
  starting transfers between devices: 15.9 us -> 0 us
  between operations: 14.2 us -> 0.65 us
    all_gather x1 -> x0, waiting for transfers between devices: 273 us -> none  [local(): lax.all_gather(train_x, TENSOR, axis=0, tiled=True)]
    pallas_call x0 -> x1, Pallas kernels: none -> 65.2 us  [local_step(): pl.pallas_call(kernel, out_shape=(jax.ShapeDtypeStruct((16, 1024), BF16),...]
    all_gather x2 -> x0, blocking collectives: 51.5 us -> none  [the longest x1 29.9 us: local(): fragment = lax.all_gather(roll_x, TENSOR, axis=1, tiled=True)]
    psum x5 -> x0, blocking collectives: 35.9 us -> none  [by_axis(): return functools.reduce(lax.psum, axes, shard)]
    dot_general x11 -> x0, matrix products: 24.7 us -> none  [the longest x1 15.6 us: local(): jnp.dot(lax.all_gather(train_x, TENSOR, axis=0, tiled=True), w_value, pre...]
    all_to_all x2 -> x0, starting transfers between devices: 15.8 us -> none  [the longest x1 9.83 us: summed_on_arrival(): lax.all_to_all(pieces, axis, split_axis=0, concat_axis=0, tiled=True)]
  transfers between devices with their start and end apart: 3 -> 0, of which waited for: 1 -> 0; matrix products, arithmetic and copies ran while one was open for 2% -> 0% of each run, Pallas kernels for 0% -> 0%
where the time goes in v1:
time: 69.7 us; the launch traced here: 69.5 us
  Pallas kernels  65.2 us (94%)
  local copies, waits for them, and re-layouts  3.75 us (5%)
    pallas_call x1, Pallas kernels, local_step(): pl.pallas_call(kernel, out_shape=(jax.ShapeDtypeStruct((16, 1024), BF16),...  65.2 us
    unnamed x2, local copies, waits for them, and re-layouts  2.6 us

profile of v1, /device:TPU:1, one launch (start us, length us, event | category | flops | bytes accessed | tf_op | source)
XLA Modules:
  0.0 69.5 jit_solution(695007582183241467)
XLA Ops:
  0.6 65.2 %shard_map.157 = (bf16[16,1024]{1,0:T(8,128)(2,1)}, f32[2,128]{1,0:T(2,128)}, f32[1,128]{1,0:T(1,128)}) custom-call(s32[16]{0:T(128)} %clen.1, s32[16]{0:T(128)} %troll.1, bf16[16,1024]{1,0:T(8,128)(2,1)} %roll_h.1, bf16[16,1024]{1,0:T(8,128)(2,1)} %q_h.1, bf16[16,256,128]{2,1,0:T(8,128)(2,1)} %ck_h.1, bf16[16,256,128]{2,1,0:T(8,128)(2,1)} %cv_h.1, ...), custom_call_target="tpu_custom_call" | custom-call | tf_op jit(solution)/shard_map/pallas_call | solution.py:395
  65.8 1.1 %slice_bitcast_fusion = f32[64]{0:T(128)} fusion(f32[1,128]{1,0:T(1,128)} %get-tuple-element.8), kind=kLoop, calls=%fused_computation | loop fusion | bytes 512 | tf_op jit(solution)/shard_map/squeeze | solution.py:443
  66.9 1.4 %copy.19 = bf16[16,1024]{1,0:T(8,128)(2,1)} copy(bf16[16,1024]{1,0:T(8,128)(2,1)} %get-tuple-element.12) | data formatting | bytes 65536
  68.3 1.2 %copy.20 = f32[2,128]{1,0:T(2,128)} copy(f32[2,128]{1,0:T(2,128)} %get-tuple-element.13) | data formatting | bytes 2048

commit v2 on v1

--- a/solution.py
+++ b/solution.py
@@ -21,24 +21,32 @@
 INVERSE = (O, XP, XM, X2, F0, FP, FM, F2)
 
 HALF = 4096
-ZROWS = 1024
-QROWS = (HALF - ZROWS) // 4
+ZROWS = 1280
 ZHALF = ZROWS // 2
-
-FROM_XM = ((XM, 0), (XM, 1), (XM, 2), (X2, 0), (X2, 2), (XM, 3), (FM, 3))
-FROM_XP = ((XP, 0), (XP, 1), (XP, 3), (X2, 1), (X2, 3), (XP, 2), (FP, 2))
-FROM_YM = ((F0, 0), (F0, 2), (FM, 0), (FM, 1), (FM, 2), (F2, 0), (F2, 2))
-FROM_YP = ((F0, 1), (F0, 3), (FP, 0), (FP, 1), (FP, 3), (F2, 1), (F2, 3))
-LINKS = (FROM_XM, FROM_XP, FROM_YM, FROM_YP)
+QUARTER = ((0, 640), (640, 640), (1280, 768), (2048, 768))
+
+
+def quarters(block, *which):
+    return tuple((block, *QUARTER[k]) for k in which)
+
+
+LINKS = (
+    quarters(XM, 0, 1, 2, 3) + quarters(X2, 0, 2) + ((F2, 3072, 512), (F2, 3584, 512)),
+    quarters(XP, 0, 1, 2, 3) + quarters(X2, 1, 3) + ((F2, 1024, 512), (F2, 2560, 512)),
+    quarters(F0, 0, 2) + quarters(FM, 0, 1, 2, 3) + ((F2, 0, 512), (F2, 1536, 512)),
+    quarters(F0, 1, 3) + quarters(FP, 0, 1, 2, 3) + ((F2, 512, 512), (F2, 2048, 512)),
+)
+ROUNDS = 8
 SENT_AS = (
-    {XM: O, X2: XM, FM: F0},
-    {XP: O, X2: XP, FP: F0},
+    {XM: O, X2: XM, F2: FM},
+    {XP: O, X2: XP, F2: FP},
     {F0: O, FM: XM, FP: XP, F2: X2},
     {F0: O, FM: XM, FP: XP, F2: X2},
 )
-Z_SEND = {0: (F0,), 1: (XM, XP), 3: (X2, FM, FP), 5: (F2,)}
-Z_TAKE = {2: (F0,), 3: (XM,), 4: (XP,), 5: (X2,), 6: (FM, FP, F2)}
-COMPLETE = {2: (F0,), 5: (XM, XP, X2), 6: (FM, FP, F2)}
+Z_SEND = {0: (F0,), 1: (XM, XP), 3: (FM, FP), 4: (X2,)}
+Z_TAKE = {2: (F0,), 3: (XM,), 4: (XP, FM), 5: (FP,), 6: (X2,)}
+FINISH = {1: (O,), 3: (F0,), 4: (XM,), 5: (XP,), 6: (FM, FP, X2), 7: (F2,)}
+AFTER_Z = ((0, 6), (1, 7))
 
 
 def dot(a, b):
@@ -53,11 +61,11 @@
 
 def kernel(
     clen, troll, roll_h, q_h, ck_h, cv_h, wk_h, wv_h, ik_h, iv_h, x_h, up_h, tt_h, adv_h,
-    attn_o, grad_o, loss_o,
-    wbuf, wv, wk, xh, up, kc, vc, q, rx, ik, iv, tt, adv, acc, pbuf, sbuf, gbuf, lmine, lbuf,
+    attn_o, whole_o,
+    wbuf, wv, wk, xh, up, kc, vc, q, rx, ik, iv, tt, adv, tt2, adv2, acc, sbuf, gbuf, lmine, lbuf,
     msg, rbuf, qs, sc, mix, snew, mt, lacc, cnt,
-    lsem, wsend, wrecv, zrecv, xsend, xrecv, rsend, rrecv, psend, precv, gsend, grecv,
-    lsend, lrecv, msend, mrecv,
+    lsem, wsend, wrecv, zrecv, xsend, xrecv, rsend, rrecv, gsend, grecv,
+    lsend, lrecv, msend, mrecv, known,
 ):
     y_hi, z, core, y_lo, x = (lax.axis_index(a) for a in AXES)
     d = y_hi * 16 + z * 2 + core
@@ -65,7 +73,6 @@
     odd = z % 2
     y = 2 * y_hi + y_lo
     y_up, y_down = (y + 1) % 4, (y + 3) % 4
-    me = (y_hi, z, core, y_lo, x)
     sibling = (y_hi, z, 1 - core, y_lo, x)
     z_up = (y_hi, (z + 1) % 8, core, y_lo, x)
     z_down = (y_hi, (z + 7) % 8, core, y_lo, x)
@@ -107,7 +114,7 @@
                 (x_h.at[:, own_half], xh.at[pl.ds(0, 256)]),
                 (tt_h, tt),
                 (adv_h, adv),
-                (up_h, up),
+                (up_h, up.at[pl.ds(0, 256)]),
                 (wk_h, wk),
                 (roll_h, rx.at[t]),
                 (ik_h.at[:, pl.ds(pl.multiple_of(t * HD, HD), HD)], ik),
@@ -122,39 +129,35 @@
         copy.start()
 
     barrier = pltpu.get_barrier_semaphore()
-
-    def greet(step, carry):
-        pl.semaphore_signal(barrier, inc=1, device_id=dp_peer(step)[1], device_id_type=MESH)
-        return carry
-
-    for block in range(1, 8):
-        pl.semaphore_signal(barrier, inc=1, device_id=peer(block), device_id_type=MESH)
-    pl.semaphore_signal(
-        barrier, inc=1, device_id=(1 - y_hi, z, core, 1 - y_lo, x), device_id_type=MESH
-    )
-    lax.fori_loop(1, 32, greet, 0)
-    pl.semaphore_wait(barrier, 39)
-
-    def quarter(k):
-        return pl.multiple_of(
-            (1 - odd) * (k * QROWS) + odd * (HALF - (k + 1) * QROWS), 64
-        )
+    neighbours = to_link + (z_up, z_down, sibling)
+
+    def tell(semaphore):
+        for device in neighbours:
+            pl.semaphore_signal(semaphore, inc=1, device_id=device, device_id_type=MESH)
+
+    def hear(semaphore):
+        pl.semaphore_wait(semaphore, len(neighbours))
+
+    tell(barrier)
+    hear(barrier)
+
+    def rows(first, length):
+        return pl.multiple_of((1 - odd) * first + odd * (HALF - first - length), 128)
 
     def link_copy(link, r):
-        block, k = LINKS[link][r]
+        block, first, length = LINKS[link][r]
         source = SENT_AS[link][block]
-        row = quarter(k)
+        row = rows(first, length)
         if source == O:
-            src = wv_h.at[pl.ds(pl.multiple_of(core * HALF + row, 64), QROWS)]
+            src = wv_h.at[pl.ds(pl.multiple_of(core * HALF + row, 128), length)]
         else:
-            src = wbuf.at[source - 1, pl.ds(row, QROWS)]
+            src = wbuf.at[source - 1, pl.ds(row, length)]
         return remote(
-            src, wbuf.at[block - 1, pl.ds(row, QROWS)], wsend, wrecv.at[link, r], to_link[link]
+            src, wbuf.at[block - 1, pl.ds(row, length)], wsend, wrecv.at[link, r], to_link[link]
         )
 
     def z_copy(block, h, base):
-        rows = pl.ds(pl.multiple_of(base + h * ZHALF, 64), ZHALF)
-        ref = wbuf.at[block - 1, rows]
+        ref = wbuf.at[block - 1, pl.ds(pl.multiple_of(base + h * ZHALF, 128), ZHALF)]
         return remote(ref, ref, wsend, zrecv.at[h, block - 1], z_up if h == 0 else z_down)
 
     z_sent = odd * (HALF - ZROWS)
@@ -162,43 +165,47 @@
 
     def issue(r):
         for link in range(4):
-            link_copy(link, r).start()
-
+            if (link, r) not in AFTER_Z:
+                link_copy(link, r).start()
+
+    issue(0)
+    issue(1)
+    tell(known.at[0])
+    exchange = [
+        remote(src, dst, xsend.at[k], xrecv.at[k], sibling)
+        for k, (src, dst) in enumerate(
+            (
+                (x_h.at[:, other_half], xh.at[pl.ds(256, 256)]),
+                (up_h, up.at[pl.ds(256, 256)]),
+                (tt_h, tt2),
+                (adv_h, adv2),
+            )
+        )
+    ]
+    for copy in exchange:
+        copy.start()
     roll_sends = [
         remote(roll_h, rx.at[t], rsend, rrecv, peer(block)) for block in range(1, 8)
     ]
-    x_copy = remote(x_h.at[:, other_half], xh.at[pl.ds(256, 256)], xsend, xrecv, sibling)
-    issue(0)
-    x_copy.start()
-    for copy in roll_sends:
-        copy.start()
-    issue(1)
 
     def product(block, row, length, first=False):
         if block == O:
-            part = wv[pl.ds(pl.multiple_of(core * HALF + row, 64), length), :]
+            part = wv[pl.ds(pl.multiple_of(core * HALF + row, 128), length), :]
         else:
             part = wbuf[block - 1, pl.ds(row, length), :]
-        new = dot(xh[:, pl.ds(pl.multiple_of(row, 64), length)], part)
+        new = dot(xh[:, pl.ds(pl.multiple_of(row, 128), length)], part)
         if first:
             acc[block] = new
         else:
             acc[block] += new
 
-    def partial_copy(block):
-        return remote(
-            acc.at[block, pl.ds(256, 256)], pbuf.at[block], psend, precv.at[block], sibling
-        )
-
     def sum_copy(block):
         return remote(
             sbuf.at[block], gbuf.at[INVERSE[block] - 1], gsend, grecv, peer(block)
         )
 
     def finish(block, first=False):
-        partial_copy(block).wait_recv()
-        values = acc[block, 0:256, :] + pbuf[block]
-        weighted = values * up[:, columns(block)].astype(F32)
+        weighted = acc[block] * up[:, columns(block)].astype(F32)
         high = weighted.astype(BF16)
         low = (weighted - high.astype(F32)).astype(BF16)
         sums = dot(mt[...], high) + dot(mt[...], low)
@@ -213,12 +220,19 @@
 
     for k in (2, 3):
         local[k].wait()
+    hear(known.at[0])
+    tell(known.at[1])
+    for k in (2, 3):
+        exchange[k].wait_recv()
     tenant = lax.broadcasted_iota(jnp.int32, (64, 128), 0)
-    hits = [
-        (tenant == jnp.broadcast_to(tt[k : k + 1, :], (64, 128))).astype(F32) for k in range(2)
-    ]
-    for k in range(2):
-        gain = jnp.broadcast_to(adv[k : k + 1, :].astype(F32), (64, 128))
+    hits = []
+    for k in range(4):
+        labels, gains = (tt, adv) if k < 2 else (tt2, adv2)
+        k2 = k % 2
+        hits.append(
+            (tenant == jnp.broadcast_to(labels[k2 : k2 + 1, :], (64, 128))).astype(F32)
+        )
+        gain = jnp.broadcast_to(gains[k2 : k2 + 1, :].astype(F32), (64, 128))
         mt[:, k * 128 : (k + 1) * 128] = (hits[k] * gain).astype(BF16)
     cnt[0:64, :] = hits[0] + hits[1]
     cnt[64:128, :] = jnp.zeros((64, 128), F32)
@@ -235,7 +249,7 @@
         return (pair == row * 8 + h).astype(F32).astype(BF16)
 
     def project():
-        for k in (5, 6, 7, 8, 9):
+        for k in (5, 6, 7, 9):
             local[k].wait()
         remote(rx.at[pl.ds(0, 7)], rx.at[pl.ds(0, 7)], rsend, rrecv, sibling).wait_recv()
         key_sum = jnp.zeros((16, HD), F32)
@@ -292,45 +306,48 @@
         for h in range(8):
             attn_o[:, h * HD : (h + 1) * HD] = dot(spread(h, True), mixed).astype(BF16)
 
-    beside = {0: project, 1: score, 2: normalise, 3: mixture}
-
-    for k in (0, 1, 4):
+    beside = {2: project, 3: score, 4: normalise, 5: mixture}
+
+    hear(known.at[1])
+    for copy in roll_sends:
+        copy.start()
+    tell(known.at[2])
+    for k in (0, 1, 4, 8):
         local[k].wait()
-    x_copy.wait_recv()
+    exchange[0].wait_recv()
     for k in range(4):
         product(O, k * 1024, 1024, k == 0)
-    partial_copy(O).start()
+    exchange[1].wait_recv()
 
     seen = {O}
-    for r in range(7):
+    for r in range(ROUNDS):
         for link in range(4):
             link_copy(link, r).wait_recv()
-        if r + 2 < 7:
+        if r + 2 < ROUNDS:
             issue(r + 2)
         for block in Z_SEND.get(r, ()):
             for h in range(2):
                 z_copy(block, h, z_sent).start()
+        if r < 4:
+            hear(known.at[r + 2])
+            if r < 3:
+                tell(known.at[r + 3])
         for link in range(4):
-            block, k = LINKS[link][r]
-            product(block, quarter(k), QROWS, block not in seen)
+            block, first, length = LINKS[link][r]
+            product(block, rows(first, length), length, block not in seen)
             seen.add(block)
         for block in Z_TAKE.get(r, ()):
             for h in range(2):
                 z_copy(block, h, z_taken).wait_recv()
-            product(block, pl.multiple_of(z_taken, 64), ZROWS)
-        for block in COMPLETE.get(r, ()):
-            partial_copy(block).start()
+        for link, later in AFTER_Z:
+            if later == r + 2:
+                link_copy(link, later).start()
+        for block in Z_TAKE.get(r, ()):
+            product(block, pl.multiple_of(z_taken, 128), ZROWS)
         if r in beside:
             beside[r]()
-        if r == 1:
-            finish(O, True)
-        if r == 3:
-            finish(F0)
-        if r == 5:
-            for block in COMPLETE[5]:
-                finish(block)
-    for block in COMPLETE[6]:
-        finish(block)
+        for block in FINISH.get(r, ()):
+            finish(block, block == O)
 
     ones = jnp.ones((8, 128), F32)
     tile_row = lax.broadcasted_iota(jnp.int32, (8, 128), 0)
@@ -365,8 +382,22 @@
     whole = rbuf[0]
     for k in range(1, 32):
         whole = whole + rbuf[k]
+    whole_o[...] = whole
+
+    for copy in exchange:
+        copy.wait_send()
+    remote(rx.at[pl.ds(0, 7)], rx.at[pl.ds(0, 7)], rsend, rrecv, sibling).wait_send()
+    remote(wbuf, wbuf, wsend, grecv, sibling).wait_send()
+    remote(gbuf, gbuf, gsend, grecv, sibling).wait_send()
+    remote(lbuf.at[pl.ds(0, 7)], lbuf.at[pl.ds(0, 7)], lsend, lrecv, sibling).wait_send()
+    remote(rbuf.at[pl.ds(0, 31)], rbuf.at[pl.ds(0, 31)], msend, mrecv, sibling).wait_send()
+
+
+def outputs(attn, whole, attn_o, grad_o, loss_o):
+    d = lax.axis_index("y_hi") * 16 + lax.axis_index("z") * 2 + lax.axis_index("core")
+    attn_o[...] = attn[...]
     divisor = jnp.maximum(whole[3:4, :], 1.0)
-    loss_o[...] = -whole[2:3, :] / divisor
+    loss_o[...] = (-whole[2:3, :] / divisor)[:, 0:TENANTS]
     lane = lax.broadcasted_iota(jnp.int32, (2, 128), 1)
     row = lax.broadcasted_iota(jnp.int32, (2, 128), 0)
     own = jnp.sum(
@@ -374,14 +405,6 @@
         axis=1, keepdims=True,
     )
     grad_o[...] = -whole[0:2, :] / own
-
-    x_copy.wait_send()
-    remote(rx.at[pl.ds(0, 7)], rx.at[pl.ds(0, 7)], rsend, rrecv, sibling).wait_send()
-    remote(wbuf, wbuf, wsend, xrecv, sibling).wait_send()
-    remote(pbuf, pbuf, psend, xrecv, sibling).wait_send()
-    remote(gbuf, gbuf, gsend, grecv, sibling).wait_send()
-    remote(lbuf.at[pl.ds(0, 7)], lbuf.at[pl.ds(0, 7)], lsend, lrecv, sibling).wait_send()
-    remote(rbuf.at[pl.ds(0, 31)], rbuf.at[pl.ds(0, 31)], msend, mrecv, sibling).wait_send()
 
 
 def local_step(
@@ -392,21 +415,20 @@
     vmem = pl.BlockSpec(memory_space=pltpu.VMEM)
     anywhere = pl.BlockSpec(memory_space=pl.ANY)
     dma = pltpu.SemaphoreType.DMA
-    attn_out, gradient, tenant_loss = pl.pallas_call(
+    attn, whole = pl.pallas_call(
         kernel,
         out_shape=(
             jax.ShapeDtypeStruct((16, 1024), BF16),
-            jax.ShapeDtypeStruct((2, 128), F32),
-            jax.ShapeDtypeStruct((1, 128), F32),
+            jax.ShapeDtypeStruct((8, 128), F32),
         ),
         in_specs=[smem, smem] + [anywhere] * 12,
-        out_specs=(vmem, vmem, vmem),
+        out_specs=(vmem, vmem),
         scratch_shapes=[
             pltpu.VMEM((7, HALF, HD), BF16),
             pltpu.VMEM((2 * HALF, HD), BF16),
             pltpu.VMEM((2 * HALF, HD), BF16),
             pltpu.VMEM((512, HALF), BF16),
-            pltpu.VMEM((256, 1024), BF16),
+            pltpu.VMEM((512, 1024), BF16),
             pltpu.VMEM((16, 256, HD), BF16),
             pltpu.VMEM((16, 256, HD), BF16),
             pltpu.VMEM((16, 1024), BF16),
@@ -415,8 +437,9 @@
             pltpu.VMEM((TENANTS, 1024), F32),
             pltpu.VMEM((2, 128), jnp.int32),
             pltpu.VMEM((2, 128), jnp.int32),
+            pltpu.VMEM((2, 128), jnp.int32),
+            pltpu.VMEM((2, 128), jnp.int32),
             pltpu.VMEM((8, 512, HD), F32),
-            pltpu.VMEM((8, 256, HD), F32),
             pltpu.VMEM((8, TENANTS, HD), F32),
             pltpu.VMEM((7, TENANTS, HD), F32),
             pltpu.VMEM((8, 128), F32),
@@ -427,11 +450,11 @@
             pltpu.VMEM((128, 256), F32),
             pltpu.VMEM((128, HD), F32),
             pltpu.VMEM((128, 128), F32),
-            pltpu.VMEM((TENANTS, 256), BF16),
+            pltpu.VMEM((TENANTS, 512), BF16),
             pltpu.VMEM((128, 128), F32),
             pltpu.VMEM((128, 128), F32),
-            dma((12,)), dma, dma((4, 7)), dma((2, 7)), dma, dma, dma, dma, dma, dma((8,)),
-            dma, dma, dma, dma, dma, dma,
+            dma((12,)), dma, dma((4, ROUNDS)), dma((2, 7)), dma((4,)), dma((4,)), dma, dma,
+            dma, dma, dma, dma, dma, dma, pltpu.SemaphoreType.REGULAR((6,)),
         ],
         compiler_params=pltpu.CompilerParams(
             collective_id=0, has_side_effects=True, vmem_limit_bytes=60 * 1024 * 1024
@@ -440,7 +463,17 @@
         cache_len, tenant_roll, roll_x, queries, cache_k, cache_v, w_key, w_value, ia3_key,
         ia3_value, train_x, upstream, tenant_train.reshape(2, 128), advantage.reshape(2, 128),
     )
-    return attn_out, gradient, tenant_loss[0, :TENANTS]
+    attn_out, gradient, tenant_loss = pl.pallas_call(
+        outputs,
+        out_shape=(
+            jax.ShapeDtypeStruct((16, 1024), BF16),
+            jax.ShapeDtypeStruct((2, 128), F32),
+            jax.ShapeDtypeStruct((1, TENANTS), F32),
+        ),
+        in_specs=[vmem, vmem],
+        out_specs=(vmem, vmem, vmem),
+    )(attn, whole)
+    return attn_out, gradient, tenant_loss.reshape(TENANTS)
 
 
 def solution(mesh):

time: 69.7 us -> 61.9 us (0.89)
  Pallas kernels: 65.2 us -> 61.1 us
  local copies, waits for them, and re-layouts: 3.75 us -> 0 us
    pallas_call x1, Pallas kernels: 65.2 us -> 59.6 us  [local_step(): pl.pallas_call(kernel, out_shape=(jax.ShapeDtypeStruct((16, 1024), BF16),...]
    unnamed x2 -> x0, local copies, waits for them, and re-layouts: 2.6 us -> none
    pallas_call x0 -> x1, Pallas kernels: none -> 1.42 us  [local_step(): pl.pallas_call(outputs, out_shape=(jax.ShapeDtypeStruct((16, 1024), BF16)...]
    squeeze x1 -> x0, local copies, waits for them, and re-layouts: 1.15 us -> none  [local_step(): return (attn_out, gradient, tenant_loss[0, :TENANTS])]
where the time goes in v2:
time: 61.9 us; the launch traced here: 61.7 us
  Pallas kernels  61.1 us (99%)
  between operations  0.64 us (1%)
    pallas_call x1, Pallas kernels, local_step(): pl.pallas_call(kernel, out_shape=(jax.ShapeDtypeStruct((16, 1024), BF16),...  59.6 us
    pallas_call x1, Pallas kernels, local_step(): pl.pallas_call(outputs, out_shape=(jax.ShapeDtypeStruct((16, 1024), BF16)...  1.42 us

profile of v2, /device:TPU:1, one launch (start us, length us, event | category | flops | bytes accessed | tf_op | source)
XLA Modules:
  0.0 61.7 jit_solution(16361064233453583631)
XLA Ops:
  0.6 59.6 %shard_map.157 = (bf16[16,1024]{1,0:T(8,128)(2,1)}, f32[8,128]{1,0:T(8,128)}) custom-call(s32[16]{0:T(128)} %clen.1, s32[16]{0:T(128)} %troll.1, bf16[16,1024]{1,0:T(8,128)(2,1)} %roll_h.1, bf16[16,1024]{1,0:T(8,128)(2,1)} %q_h.1, bf16[16,256,128]{2,1,0:T(8,128)(2,1)} %ck_h.1, bf16[16,256,128]{2,1,0:T(8,128)(2,1)} %cv_h.1, bf16[8192,128]{1,0:T(8,128)(2,1)} %wk_h.1, ...), custom_call_target="tpu_custom_call" | custom-call | tf_op jit(solution)/shard_map/pallas_call | solution.py:418
  60.3 1.4 %shard_map.158 = (bf16[16,1024]{1,0:T(8,128)(2,1)}, f32[2,128]{1,0:T(2,128)}, f32[1,64]{1,0:T(1,128)}) custom-call(bf16[16,1024]{1,0:T(8,128)(2,1)} %get-tuple-element.8.attn, f32[8,128]{1,0:T(8,128)} %get-tuple-element.9.whole), custom_call_target="tpu_custom_call" | custom-call | tf_op jit(solution)/shard_map/pallas_call | solution.py:466

commit v3 on v2

--- a/solution.py
+++ b/solution.py
@@ -44,8 +44,17 @@
     {F0: O, FM: XM, FP: XP, F2: X2},
 )
 Z_SEND = {0: (F0,), 1: (XM, XP), 3: (FM, FP), 4: (X2,)}
-Z_TAKE = {2: (F0,), 3: (XM,), 4: (XP, FM), 5: (FP,), 6: (X2,)}
-FINISH = {1: (O,), 3: (F0,), 4: (XM,), 5: (XP,), 6: (FM, FP, X2), 7: (F2,)}
+Z_TAKE = {2: (F0,), 4: (XM, XP, FM), 5: (FP,), 6: (X2,)}
+PRODUCTS = {
+    1: (((O, F0), 0, 1280), ((XM, XP), 0, 640), ((O, F0), 1280, 1536), ((XM, XP), 640, 640)),
+    2: (((XM, XP), 1280, 768), ((FM, FP), 0, 640), ((O, F0), 2816, 1280)),
+    3: (((XM, XP), 2048, 768), ((FM, FP), 640, 640)),
+    4: (((X2,), 0, 1280), ((FM, FP), 1280, 768), ((XM, XP), 2816, 1280)),
+    5: (((X2,), 1280, 1536), ((FM, FP), 2048, 768), ((FM, FP), 2816, 1280)),
+    6: (((F2,), 0, 1536), ((F2,), 3072, 512), ((X2,), 2816, 1280)),
+    7: (((F2,), 1536, 1536), ((F2,), 3584, 512)),
+}
+FINISH = {3: (O, F0), 4: (XM,), 5: (XP,), 6: (FM, FP, X2), 7: (F2,)}
 AFTER_Z = ((0, 6), (1, 7))
 
 
@@ -68,7 +77,6 @@
     lsend, lrecv, msend, mrecv, known,
 ):
     y_hi, z, core, y_lo, x = (lax.axis_index(a) for a in AXES)
-    d = y_hi * 16 + z * 2 + core
     t = y_lo * 4 + x
     odd = z % 2
     y = 2 * y_hi + y_lo
@@ -94,9 +102,13 @@
         py, px = place(block)
         return pl.ds(pl.multiple_of((py * 4 + px) * HD, HD), HD)
 
-    def dp_peer(step):
-        other = (d + step) % 32
-        return other, (other // 16, (other // 2) % 8, other % 2, y_lo, x)
+    def plane_peer(step):
+        other = (y * 4 + x + step) % 16
+        return other, (other // 8, z, core, (other // 4) % 2, other % 4)
+
+    def column_peer(step):
+        other = (z * 2 + core + step) % 16
+        return other, (y_hi, other // 2, other % 2, y_lo, x)
 
     def remote(src, dst, send, recv, device):
         return pltpu.make_async_remote_copy(
@@ -188,21 +200,35 @@
         remote(roll_h, rx.at[t], rsend, rrecv, peer(block)) for block in range(1, 8)
     ]
 
-    def product(block, row, length, first=False):
+    def part_of(block, row, length):
         if block == O:
-            part = wv[pl.ds(pl.multiple_of(core * HALF + row, 128), length), :]
-        else:
-            part = wbuf[block - 1, pl.ds(row, length), :]
-        new = dot(xh[:, pl.ds(pl.multiple_of(row, 128), length)], part)
-        if first:
-            acc[block] = new
-        else:
-            acc[block] += new
-
-    def sum_copy(block):
-        return remote(
-            sbuf.at[block], gbuf.at[INVERSE[block] - 1], gsend, grecv, peer(block)
-        )
+            return wv[pl.ds(pl.multiple_of(core * HALF + row, 128), length), :]
+        return wbuf[block - 1, pl.ds(row, length), :]
+
+    def product(blocks, first, length, new):
+        row = rows(first, length)
+        parts = [part_of(block, row, length) for block in blocks]
+        both = parts[0] if len(parts) == 1 else jnp.concatenate(parts, axis=1)
+        result = dot(xh[:, pl.ds(row, length)], both)
+        for k, block in enumerate(blocks):
+            if new:
+                acc[block] = result[:, k * HD : (k + 1) * HD]
+            else:
+                acc[block] += result[:, k * HD : (k + 1) * HD]
+
+    def sum_copies(block):
+        copies = []
+        for k, high in enumerate((y_hi, 1 - y_hi)):
+            slot = INVERSE[block] + 8 * k
+            if slot > 0:
+                py, px = place(block)
+                copies.append(
+                    remote(
+                        sbuf.at[block, pl.ds(pl.multiple_of(32 * high, 32), 32)],
+                        gbuf.at[slot - 1], gsend, grecv, (high, z, core, py, px),
+                    )
+                )
+        return copies
 
     def finish(block, first=False):
         weighted = acc[block] * up[:, columns(block)].astype(F32)
@@ -210,33 +236,32 @@
         low = (weighted - high.astype(F32)).astype(BF16)
         sums = dot(mt[...], high) + dot(mt[...], low)
         sbuf[block] = sums
-        if block != O:
-            sum_copy(block).start()
+        for copy in sum_copies(block):
+            copy.start()
         part = sums * iv[:, columns(block)]
         if first:
             lacc[0:64, :] = part
         else:
             lacc[0:64, :] += part
 
-    for k in (2, 3):
-        local[k].wait()
-    hear(known.at[0])
-    tell(known.at[1])
-    for k in (2, 3):
-        exchange[k].wait_recv()
-    tenant = lax.broadcasted_iota(jnp.int32, (64, 128), 0)
-    hits = []
-    for k in range(4):
-        labels, gains = (tt, adv) if k < 2 else (tt2, adv2)
-        k2 = k % 2
-        hits.append(
-            (tenant == jnp.broadcast_to(labels[k2 : k2 + 1, :], (64, 128))).astype(F32)
-        )
-        gain = jnp.broadcast_to(gains[k2 : k2 + 1, :].astype(F32), (64, 128))
-        mt[:, k * 128 : (k + 1) * 128] = (hits[k] * gain).astype(BF16)
-    cnt[0:64, :] = hits[0] + hits[1]
-    cnt[64:128, :] = jnp.zeros((64, 128), F32)
-    lacc[64:128, :] = jnp.zeros((64, 128), F32)
+    def table():
+        for k in (2, 3):
+            local[k].wait()
+        for k in (2, 3):
+            exchange[k].wait_recv()
+        tenant = lax.broadcasted_iota(jnp.int32, (64, 128), 0)
+        hits = []
+        for k in range(4):
+            labels, gains = (tt, adv) if k < 2 else (tt2, adv2)
+            k2 = k % 2
+            hits.append(
+                (tenant == jnp.broadcast_to(labels[k2 : k2 + 1, :], (64, 128))).astype(F32)
+            )
+            gain = jnp.broadcast_to(gains[k2 : k2 + 1, :].astype(F32), (64, 128))
+            mt[:, k * 128 : (k + 1) * 128] = (hits[k] * gain).astype(BF16)
+        cnt[0:64, :] = hits[0] + hits[1]
+        cnt[64:128, :] = jnp.zeros((64, 128), F32)
+        lacc[64:128, :] = jnp.zeros((64, 128), F32)
 
     scale = 1.0 / jnp.sqrt(F32(HD))
 
@@ -306,20 +331,19 @@
         for h in range(8):
             attn_o[:, h * HD : (h + 1) * HD] = dot(spread(h, True), mixed).astype(BF16)
 
+    ones = jnp.ones((8, 128), F32)
+    tile_row = lax.broadcasted_iota(jnp.int32, (8, 128), 0)
+
+    def loss_and_count():
+        loss_row = exact_dot(ones, lacc[...], ((1,), (1,)))
+        count_row = exact_dot(ones, cnt[...], ((1,), (1,)))
+        return jnp.where(tile_row == 2, loss_row, jnp.where(tile_row == 3, count_row, 0.0))
+
     beside = {2: project, 3: score, 4: normalise, 5: mixture}
 
-    hear(known.at[1])
-    for copy in roll_sends:
-        copy.start()
-    tell(known.at[2])
-    for k in (0, 1, 4, 8):
-        local[k].wait()
-    exchange[0].wait_recv()
-    for k in range(4):
-        product(O, k * 1024, 1024, k == 0)
-    exchange[1].wait_recv()
-
-    seen = {O}
+    hear(known.at[0])
+    tell(known.at[1])
+    seen = set()
     for r in range(ROUNDS):
         for link in range(4):
             link_copy(link, r).wait_recv()
@@ -328,59 +352,61 @@
         for block in Z_SEND.get(r, ()):
             for h in range(2):
                 z_copy(block, h, z_sent).start()
-        if r < 4:
-            hear(known.at[r + 2])
-            if r < 3:
-                tell(known.at[r + 3])
-        for link in range(4):
-            block, first, length = LINKS[link][r]
-            product(block, rows(first, length), length, block not in seen)
-            seen.add(block)
+        if r < 3:
+            hear(known.at[r + 1])
+            if r < 2:
+                tell(known.at[r + 2])
+        if r == 0:
+            for copy in roll_sends:
+                copy.start()
+            table()
+            for k in (0, 1, 4, 8):
+                local[k].wait()
+        if r == 1:
+            exchange[0].wait_recv()
+            exchange[1].wait_recv()
         for block in Z_TAKE.get(r, ()):
             for h in range(2):
                 z_copy(block, h, z_taken).wait_recv()
         for link, later in AFTER_Z:
             if later == r + 2:
                 link_copy(link, later).start()
-        for block in Z_TAKE.get(r, ()):
-            product(block, pl.multiple_of(z_taken, 128), ZROWS)
+        for blocks, first, length in PRODUCTS.get(r, ()):
+            product(blocks, first, length, blocks[0] not in seen)
+            seen.update(blocks)
         if r in beside:
             beside[r]()
         for block in FINISH.get(r, ()):
-            finish(block, block == O)
-
-    ones = jnp.ones((8, 128), F32)
-    tile_row = lax.broadcasted_iota(jnp.int32, (8, 128), 0)
-    loss_row = exact_dot(ones, lacc[...], ((1,), (1,)))
-    count_row = exact_dot(ones, cnt[...], ((1,), (1,)))
-    mine = jnp.where(tile_row == 2, loss_row, jnp.where(tile_row == 3, count_row, 0.0))
+            finish(block, block in (O, F2))
+        if r == ROUNDS - 2:
+            lmine[...] = loss_and_count()
+
+    group = y * 4 + x
+    mine = lmine[...] + jnp.where(tile_row == 2, exact_dot(ones, lacc[...], ((1,), (1,))), 0.0)
     lmine[...] = mine
-    for block in range(1, 8):
-        remote(lmine, lbuf.at[t], lsend, lrecv, peer(block)).start()
-    lbuf[t] = mine
+    for step in range(1, 16):
+        remote(lmine, lbuf.at[group], lsend, lrecv, plane_peer(step)[1]).start()
+    lbuf[group] = mine
 
     remote(gbuf, gbuf, gsend, grecv, sibling).wait_recv()
-    total = sbuf[O]
-    for k in range(7):
+    total = sbuf[O, pl.ds(pl.multiple_of(32 * y_hi, 32), 32), :]
+    for k in range(15):
         total = total + gbuf[k]
-    remote(lbuf.at[pl.ds(0, 7)], lbuf.at[pl.ds(0, 7)], lsend, lrecv, sibling).wait_recv()
-    group = lbuf[0]
-    for k in range(1, 8):
-        group = group + lbuf[k]
-    for k in range(32):
-        msg[k] = group
+    remote(lbuf.at[pl.ds(0, 15)], lbuf.at[pl.ds(0, 15)], lsend, lrecv, sibling).wait_recv()
+    plane = lbuf[0]
+    for k in range(1, 16):
+        plane = plane + lbuf[k]
+    for k in range(16):
+        msg[k] = plane
         msg[k, 0:2, :] = total[2 * k : 2 * k + 2, :]
-
-    def scatter(step, carry):
-        other, device = dp_peer(step)
-        remote(msg.at[other], rbuf.at[d], msend, mrecv, device).start()
-        return carry
-
-    lax.fori_loop(1, 32, scatter, 0)
-    rbuf[d] = msg[d]
-    remote(rbuf.at[pl.ds(0, 31)], rbuf.at[pl.ds(0, 31)], msend, mrecv, sibling).wait_recv()
+    own = z * 2 + core
+    for step in range(1, 16):
+        other, device = column_peer(step)
+        remote(msg.at[other], rbuf.at[own], msend, mrecv, device).start()
+    rbuf[own] = msg[own]
+    remote(rbuf.at[pl.ds(0, 15)], rbuf.at[pl.ds(0, 15)], msend, mrecv, sibling).wait_recv()
     whole = rbuf[0]
-    for k in range(1, 32):
+    for k in range(1, 16):
         whole = whole + rbuf[k]
     whole_o[...] = whole
 
@@ -389,8 +415,8 @@
     remote(rx.at[pl.ds(0, 7)], rx.at[pl.ds(0, 7)], rsend, rrecv, sibling).wait_send()
     remote(wbuf, wbuf, wsend, grecv, sibling).wait_send()
     remote(gbuf, gbuf, gsend, grecv, sibling).wait_send()
-    remote(lbuf.at[pl.ds(0, 7)], lbuf.at[pl.ds(0, 7)], lsend, lrecv, sibling).wait_send()
-    remote(rbuf.at[pl.ds(0, 31)], rbuf.at[pl.ds(0, 31)], msend, mrecv, sibling).wait_send()
+    remote(lbuf.at[pl.ds(0, 15)], lbuf.at[pl.ds(0, 15)], lsend, lrecv, sibling).wait_send()
+    remote(rbuf.at[pl.ds(0, 15)], rbuf.at[pl.ds(0, 15)], msend, mrecv, sibling).wait_send()
 
 
 def outputs(attn, whole, attn_o, grad_o, loss_o):
@@ -441,11 +467,11 @@
             pltpu.VMEM((2, 128), jnp.int32),
             pltpu.VMEM((8, 512, HD), F32),
             pltpu.VMEM((8, TENANTS, HD), F32),
-            pltpu.VMEM((7, TENANTS, HD), F32),
+            pltpu.VMEM((15, 32, HD), F32),
             pltpu.VMEM((8, 128), F32),
-            pltpu.VMEM((8, 8, 128), F32),
-            pltpu.VMEM((32, 8, 128), F32),
-            pltpu.VMEM((32, 8, 128), F32),
+            pltpu.VMEM((16, 8, 128), F32),
+            pltpu.VMEM((16, 8, 128), F32),
+            pltpu.VMEM((16, 8, 128), F32),
             pltpu.VMEM((128, HD), F32),
             pltpu.VMEM((128, 256), F32),
             pltpu.VMEM((128, HD), F32),
@@ -454,7 +480,7 @@
             pltpu.VMEM((128, 128), F32),
             pltpu.VMEM((128, 128), F32),
             dma((12,)), dma, dma((4, ROUNDS)), dma((2, 7)), dma((4,)), dma((4,)), dma, dma,
-            dma, dma, dma, dma, dma, dma, pltpu.SemaphoreType.REGULAR((6,)),
+            dma, dma, dma, dma, dma, dma, pltpu.SemaphoreType.REGULAR((4,)),
         ],
         compiler_params=pltpu.CompilerParams(
             collective_id=0, has_side_effects=True, vmem_limit_bytes=60 * 1024 * 1024

time: 61.9 us -> 60.9 us (0.984)
  Pallas kernels: 61.1 us -> 60.1 us
    pallas_call x1, Pallas kernels: 59.6 us -> 58.7 us  [local_step(): pl.pallas_call(kernel, out_shape=(jax.ShapeDtypeStruct((16, 1024), BF16),...]
where the time goes in v3:
time: 60.9 us; the launch traced here: 60.7 us
  Pallas kernels  60.1 us (99%)
  between operations  0.64 us (1%)
    pallas_call x1, Pallas kernels, local_step(): pl.pallas_call(kernel, out_shape=(jax.ShapeDtypeStruct((16, 1024), BF16),...  58.7 us
    pallas_call x1, Pallas kernels, local_step(): pl.pallas_call(outputs, out_shape=(jax.ShapeDtypeStruct((16, 1024), BF16)...  1.42 us

profile of v3, /device:TPU:1, one launch (start us, length us, event | category | flops | bytes accessed | tf_op | source)
XLA Modules:
  0.0 60.7 jit_solution(15958619356247518793)
XLA Ops:
  0.6 58.7 %shard_map.157 = (bf16[16,1024]{1,0:T(8,128)(2,1)}, f32[8,128]{1,0:T(8,128)}) custom-call(s32[16]{0:T(128)} %clen.1, s32[16]{0:T(128)} %troll.1, bf16[16,1024]{1,0:T(8,128)(2,1)} %roll_h.1, bf16[16,1024]{1,0:T(8,128)(2,1)} %q_h.1, bf16[16,256,128]{2,1,0:T(8,128)(2,1)} %ck_h.1, bf16[16,256,128]{2,1,0:T(8,128)(2,1)} %cv_h.1, bf16[8192,128]{1,0:T(8,128)(2,1)} %wk_h.1, ...), custom_call_target="tpu_custom_call" | custom-call | tf_op jit(solution)/shard_map/pallas_call | solution.py:444
  59.3 1.4 %shard_map.158 = (bf16[16,1024]{1,0:T(8,128)(2,1)}, f32[2,128]{1,0:T(2,128)}, f32[1,64]{1,0:T(1,128)}) custom-call(bf16[16,1024]{1,0:T(8,128)(2,1)} %get-tuple-element.8.attn, f32[8,128]{1,0:T(8,128)} %get-tuple-element.9.whole), custom_call_target="tpu_custom_call" | custom-call | tf_op jit(solution)/shard_map/pallas_call | solution.py:492

commit v4 on v3

--- a/solution.py
+++ b/solution.py
@@ -18,7 +18,6 @@
 
 O, XM, XP, X2, F0, FM, FP, F2 = range(8)
 SHIFT = ((0, 0), (0, 3), (0, 1), (0, 2), (1, 0), (1, 3), (1, 1), (1, 2))
-INVERSE = (O, XP, XM, X2, F0, FP, FM, F2)
 
 HALF = 4096
 ZROWS = 1280
@@ -71,10 +70,10 @@
 def kernel(
     clen, troll, roll_h, q_h, ck_h, cv_h, wk_h, wv_h, ik_h, iv_h, x_h, up_h, tt_h, adv_h,
     attn_o, whole_o,
-    wbuf, wv, wk, xh, up, kc, vc, q, rx, ik, iv, tt, adv, tt2, adv2, acc, sbuf, gbuf, lmine, lbuf,
-    msg, rbuf, qs, sc, mix, snew, mt, lacc, cnt,
+    wbuf, wv, wk, xh, up, kc, vc, q, rx, ik, iv, tt, adv, tt2, adv2, acc, zmsg, zbuf, fmsg, fbuf, lmine,
+    msg, rbuf, smsg, sbuf, qs, sc, mix, snew, mt, lacc, cnt,
     lsem, wsend, wrecv, zrecv, xsend, xrecv, rsend, rrecv, gsend, grecv,
-    lsend, lrecv, msend, mrecv, known,
+    msend, mrecv, ssend, srecv, known,
 ):
     y_hi, z, core, y_lo, x = (lax.axis_index(a) for a in AXES)
     t = y_lo * 4 + x
@@ -102,13 +101,9 @@
         py, px = place(block)
         return pl.ds(pl.multiple_of((py * 4 + px) * HD, HD), HD)
 
-    def plane_peer(step):
-        other = (y * 4 + x + step) % 16
-        return other, (other // 8, z, core, (other // 4) % 2, other % 4)
-
-    def column_peer(step):
-        other = (z * 2 + core + step) % 16
-        return other, (y_hi, other // 2, other % 2, y_lo, x)
+    def z_peer(step):
+        other = (z + step) % 8
+        return other, (y_hi, other, core, y_lo, x)
 
     def remote(src, dst, send, recv, device):
         return pltpu.make_async_remote_copy(
@@ -196,9 +191,26 @@
     ]
     for copy in exchange:
         copy.start()
-    roll_sends = [
-        remote(roll_h, rx.at[t], rsend, rrecv, peer(block)) for block in range(1, 8)
-    ]
+    beside_y = (y_hi, z, core, 1 - y_lo, x)
+    RELAY = (
+        ((0, O, 0, 1024), (1, O, 0, 1024), (4, O, 0, 1024)),
+        ((0, XM, 0, 512), (1, XP, 512, 512), (0, F0, 0, 1024), (1, F0, 0, 1024)),
+        ((4, X2, 0, 1024),),
+    )
+
+    def relay(step):
+        copies = []
+        for k, (to, block, first, width) in enumerate(RELAY[step]):
+            py, px = place(block)
+            here = py * 4 + px
+            slot = rx.at[here, :, pl.ds(first, width)]
+            source = roll_h if block == O else slot
+            device = beside_y if to == 4 else to_link[to]
+            copies.append(remote(source, slot, rsend, rrecv.at[3 * step + step // 2 + k], device))
+        return copies
+
+    for copy in relay(0):
+        copy.start()
 
     def part_of(block, row, length):
         if block == O:
@@ -216,33 +228,61 @@
             else:
                 acc[block] += result[:, k * HD : (k + 1) * HD]
 
-    def sum_copies(block):
+    def z_copies(block):
         copies = []
-        for k, high in enumerate((y_hi, 1 - y_hi)):
-            slot = INVERSE[block] + 8 * k
-            if slot > 0:
-                py, px = place(block)
-                copies.append(
-                    remote(
-                        sbuf.at[block, pl.ds(pl.multiple_of(32 * high, 32), 32)],
-                        gbuf.at[slot - 1], gsend, grecv, (high, z, core, py, px),
-                    )
-                )
+        for step in range(1, 8):
+            other, device = z_peer(step)
+            if block == F2:
+                pair = fmsg.at[other], fbuf.at[z]
+            else:
+                pair = zmsg.at[block, other], zbuf.at[block, z]
+            copies.append(remote(*pair, gsend, grecv.at[block], device))
         return copies
 
-    def finish(block, first=False):
+    def fold(block):
         weighted = acc[block] * up[:, columns(block)].astype(F32)
         high = weighted.astype(BF16)
         low = (weighted - high.astype(F32)).astype(BF16)
-        sums = dot(mt[...], high) + dot(mt[...], low)
-        sbuf[block] = sums
-        for copy in sum_copies(block):
-            copy.start()
+        return dot(mt[...], high) + dot(mt[...], low)
+
+    def finish(block, first=False):
+        sums = fold(block)
         part = sums * iv[:, columns(block)]
-        if first:
+        for k in range(8):
+            if block == F2:
+                fmsg[k, 0:4, :] = sums[4 * k : 4 * k + 4, :]
+                fmsg[k, 4:8, :] = sums[32 + 4 * k : 36 + 4 * k, :]
+            else:
+                zmsg[block, k, 0:4, :] = sums[4 * k : 4 * k + 4, :]
+                zmsg[block, k, 4:8, :] = sums[32 + 4 * k : 36 + 4 * k, :]
+        if block == F2:
+            lacc[0:64, :] = part
+            mine = lmine[...] + jnp.where(
+                tile_row == 4, exact_dot(ones, lacc[...], ((1,), (1,))), 0.0
+            )
+            for k in range(8):
+                fmsg[k, 8:16, :] = mine
+        elif first:
             lacc[0:64, :] = part
         else:
             lacc[0:64, :] += part
+        for copy in z_copies(block):
+            copy.start()
+        if block == F2:
+            fbuf[z] = fmsg[z]
+        else:
+            zbuf[block, z] = zmsg[block, z]
+
+    def over_z(block):
+        buf = fbuf if block == F2 else zbuf.at[block]
+        some = buf.at[pl.ds(0, 7)]
+        remote(some, some, gsend, grecv.at[block], sibling).wait_recv()
+        total = buf[0]
+        for k in range(1, 8):
+            total = total + buf[k]
+        for k in range(2):
+            msg[block, k, 0:4, :] = total[4 * k : 4 * k + 4, :]
+        return total
 
     def table():
         for k in (2, 3):
@@ -276,7 +316,7 @@
     def project():
         for k in (5, 6, 7, 9):
             local[k].wait()
-        remote(rx.at[pl.ds(0, 7)], rx.at[pl.ds(0, 7)], rsend, rrecv, sibling).wait_recv()
+        relay(2)[0].wait_recv()
         key_sum = jnp.zeros((16, HD), F32)
         value_sum = jnp.zeros((16, HD), F32)
         for k in range(8):
@@ -337,7 +377,7 @@
     def loss_and_count():
         loss_row = exact_dot(ones, lacc[...], ((1,), (1,)))
         count_row = exact_dot(ones, cnt[...], ((1,), (1,)))
-        return jnp.where(tile_row == 2, loss_row, jnp.where(tile_row == 3, count_row, 0.0))
+        return jnp.where(tile_row == 4, loss_row, jnp.where(tile_row == 5, count_row, 0.0))
 
     beside = {2: project, 3: score, 4: normalise, 5: mixture}
 
@@ -356,9 +396,12 @@
             hear(known.at[r + 1])
             if r < 2:
                 tell(known.at[r + 2])
+        if r < 2:
+            for copy in relay(r):
+                copy.wait_recv()
+            for copy in relay(r + 1):
+                copy.start()
         if r == 0:
-            for copy in roll_sends:
-                copy.start()
             table()
             for k in (0, 1, 4, 8):
                 local[k].wait()
@@ -377,60 +420,61 @@
         if r in beside:
             beside[r]()
         for block in FINISH.get(r, ()):
-            finish(block, block in (O, F2))
+            finish(block, block == O)
         if r == ROUNDS - 2:
             lmine[...] = loss_and_count()
-
+        if r == ROUNDS - 1:
+            for block in range(F2):
+                over_z(block)
+
+    last = over_z(F2)
+    for block in range(8):
+        for k in range(2):
+            msg[block, k, 4:8, :] = last[12:16, :]
     group = y * 4 + x
-    mine = lmine[...] + jnp.where(tile_row == 2, exact_dot(ones, lacc[...], ((1,), (1,))), 0.0)
-    lmine[...] = mine
-    for step in range(1, 16):
-        remote(lmine, lbuf.at[group], lsend, lrecv, plane_peer(step)[1]).start()
-    lbuf[group] = mine
-
-    remote(gbuf, gbuf, gsend, grecv, sibling).wait_recv()
-    total = sbuf[O, pl.ds(pl.multiple_of(32 * y_hi, 32), 32), :]
-    for k in range(15):
-        total = total + gbuf[k]
-    remote(lbuf.at[pl.ds(0, 15)], lbuf.at[pl.ds(0, 15)], lsend, lrecv, sibling).wait_recv()
-    plane = lbuf[0]
+    for block in range(8):
+        py, px = place(block)
+        for k, high in enumerate((y_hi, 1 - y_hi)):
+            if block + k > 0:
+                remote(
+                    msg.at[block, high], rbuf.at[group], msend, mrecv, (high, z, core, py, px)
+                ).start()
+    rbuf[group] = msg[O, y_hi]
+    some = rbuf.at[pl.ds(0, 15)]
+    remote(some, some, msend, mrecv, sibling).wait_recv()
+    plane = rbuf[0]
     for k in range(1, 16):
-        plane = plane + lbuf[k]
-    for k in range(16):
-        msg[k] = plane
-        msg[k, 0:2, :] = total[2 * k : 2 * k + 2, :]
-    own = z * 2 + core
-    for step in range(1, 16):
-        other, device = column_peer(step)
-        remote(msg.at[other], rbuf.at[own], msend, mrecv, device).start()
-    rbuf[own] = msg[own]
-    remote(rbuf.at[pl.ds(0, 15)], rbuf.at[pl.ds(0, 15)], msend, mrecv, sibling).wait_recv()
-    whole = rbuf[0]
-    for k in range(1, 16):
-        whole = whole + rbuf[k]
+        plane = plane + rbuf[k]
+    smsg[...] = plane
+    across = remote(smsg, sbuf, ssend, srecv, sibling)
+    across.start()
+    across.wait_recv()
+    whole = plane + sbuf[...]
     whole_o[...] = whole
 
     for copy in exchange:
         copy.wait_send()
-    remote(rx.at[pl.ds(0, 7)], rx.at[pl.ds(0, 7)], rsend, rrecv, sibling).wait_send()
-    remote(wbuf, wbuf, wsend, grecv, sibling).wait_send()
-    remote(gbuf, gbuf, gsend, grecv, sibling).wait_send()
-    remote(lbuf.at[pl.ds(0, 15)], lbuf.at[pl.ds(0, 15)], lsend, lrecv, sibling).wait_send()
+    remote(rx.at[pl.ds(0, 7)], rx.at[pl.ds(0, 7)], rsend, srecv, sibling).wait_send()
+    remote(wbuf, wbuf, wsend, srecv, sibling).wait_send()
+    across.wait_send()
+    remote(zbuf.at[pl.ds(0, 7), pl.ds(0, 7)], zbuf.at[pl.ds(0, 7), pl.ds(0, 7)], gsend, srecv, sibling).wait_send()
+    remote(fbuf.at[pl.ds(0, 7)], fbuf.at[pl.ds(0, 7)], gsend, srecv, sibling).wait_send()
     remote(rbuf.at[pl.ds(0, 15)], rbuf.at[pl.ds(0, 15)], msend, mrecv, sibling).wait_send()
 
 
 def outputs(attn, whole, attn_o, grad_o, loss_o):
-    d = lax.axis_index("y_hi") * 16 + lax.axis_index("z") * 2 + lax.axis_index("core")
+    core = lax.axis_index("core")
+    d = lax.axis_index("y_hi") * 16 + lax.axis_index("z") * 2 + core
     attn_o[...] = attn[...]
-    divisor = jnp.maximum(whole[3:4, :], 1.0)
-    loss_o[...] = (-whole[2:3, :] / divisor)[:, 0:TENANTS]
+    divisor = jnp.maximum(whole[5:6, :], 1.0)
+    loss_o[...] = (-whole[4:5, :] / divisor)[:, 0:TENANTS]
     lane = lax.broadcasted_iota(jnp.int32, (2, 128), 1)
     row = lax.broadcasted_iota(jnp.int32, (2, 128), 0)
     own = jnp.sum(
         jnp.where(lane == 2 * d + row, jnp.broadcast_to(divisor, (2, 128)), 0.0),
         axis=1, keepdims=True,
     )
-    grad_o[...] = -whole[0:2, :] / own
+    grad_o[...] = -jnp.where(core == 0, whole[0:2, :], whole[2:4, :]) / own
 
 
 def local_step(
@@ -466,12 +510,15 @@
             pltpu.VMEM((2, 128), jnp.int32),
             pltpu.VMEM((2, 128), jnp.int32),
             pltpu.VMEM((8, 512, HD), F32),
-            pltpu.VMEM((8, TENANTS, HD), F32),
-            pltpu.VMEM((15, 32, HD), F32),
+            pltpu.VMEM((7, 8, 8, HD), F32),
+            pltpu.VMEM((7, 8, 8, HD), F32),
+            pltpu.VMEM((8, 16, HD), F32),
+            pltpu.VMEM((8, 16, HD), F32),
             pltpu.VMEM((8, 128), F32),
-            pltpu.VMEM((16, 8, 128), F32),
-            pltpu.VMEM((16, 8, 128), F32),
-            pltpu.VMEM((16, 8, 128), F32),
+            pltpu.VMEM((8, 2, 8, HD), F32),
+            pltpu.VMEM((16, 8, HD), F32),
+            pltpu.VMEM((8, HD), F32),
+            pltpu.VMEM((8, HD), F32),
             pltpu.VMEM((128, HD), F32),
             pltpu.VMEM((128, 256), F32),
             pltpu.VMEM((128, HD), F32),
@@ -479,8 +526,8 @@
             pltpu.VMEM((TENANTS, 512), BF16),
             pltpu.VMEM((128, 128), F32),
             pltpu.VMEM((128, 128), F32),
-            dma((12,)), dma, dma((4, ROUNDS)), dma((2, 7)), dma((4,)), dma((4,)), dma, dma,
-            dma, dma, dma, dma, dma, dma, pltpu.SemaphoreType.REGULAR((4,)),
+            dma((12,)), dma, dma((4, ROUNDS)), dma((2, 7)), dma((4,)), dma((4,)), dma, dma((8,)),
+            dma, dma((8,)), dma, dma, dma, dma, pltpu.SemaphoreType.REGULAR((4,)),
         ],
         compiler_params=pltpu.CompilerParams(
             collective_id=0, has_side_effects=True, vmem_limit_bytes=60 * 1024 * 1024

time: 60.9 us -> 63.4 us (1.041)
  Pallas kernels: 60.1 us -> 62.6 us
    pallas_call x1, Pallas kernels: 58.7 us -> 61.2 us  [local_step(): pl.pallas_call(kernel, out_shape=(jax.ShapeDtypeStruct((16, 1024), BF16),...]
where the time goes in v4:
time: 63.4 us; the launch traced here: 63.2 us
  Pallas kernels  62.6 us (99%)
  between operations  0.64 us (1%)
    pallas_call x1, Pallas kernels, local_step(): pl.pallas_call(kernel, out_shape=(jax.ShapeDtypeStruct((16, 1024), BF16),...  61.2 us
    pallas_call x1, Pallas kernels, local_step(): pl.pallas_call(outputs, out_shape=(jax.ShapeDtypeStruct((16, 1024), BF16)...  1.42 us

profile of v4, /device:TPU:1, one launch (start us, length us, event | category | flops | bytes accessed | tf_op | source)
XLA Modules:
  0.0 63.2 jit_solution(2608734821496809317)
XLA Ops:
  0.6 61.2 %shard_map.157 = (bf16[16,1024]{1,0:T(8,128)(2,1)}, f32[8,128]{1,0:T(8,128)}) custom-call(s32[16]{0:T(128)} %clen.1, s32[16]{0:T(128)} %troll.1, bf16[16,1024]{1,0:T(8,128)(2,1)} %roll_h.1, bf16[16,1024]{1,0:T(8,128)(2,1)} %q_h.1, bf16[16,256,128]{2,1,0:T(8,128)(2,1)} %ck_h.1, bf16[16,256,128]{2,1,0:T(8,128)(2,1)} %cv_h.1, bf16[8192,128]{1,0:T(8,128)(2,1)} %wk_h.1, ...), custom_call_target="tpu_custom_call" | custom-call | tf_op jit(solution)/shard_map/pallas_call | solution.py:488
  61.8 1.4 %shard_map.158 = (bf16[16,1024]{1,0:T(8,128)(2,1)}, f32[2,128]{1,0:T(2,128)}, f32[1,64]{1,0:T(1,128)}) custom-call(bf16[16,1024]{1,0:T(8,128)(2,1)} %get-tuple-element.8.attn, f32[8,128]{1,0:T(8,128)} %get-tuple-element.9.whole), custom_call_target="tpu_custom_call" | custom-call | tf_op jit(solution)/shard_map/pallas_call | solution.py:539

commit v5 on v3

--- a/solution.py
+++ b/solution.py
@@ -137,9 +137,6 @@
             )
         )
     ]
-    for copy in local:
-        copy.start()
-
     barrier = pltpu.get_barrier_semaphore()
     neighbours = to_link + (z_up, z_down, sibling)
 
@@ -151,6 +148,8 @@
         pl.semaphore_wait(semaphore, len(neighbours))
 
     tell(barrier)
+    for copy in local:
+        copy.start()
     hear(barrier)
 
     def rows(first, length):
@@ -196,9 +195,26 @@
     ]
     for copy in exchange:
         copy.start()
-    roll_sends = [
-        remote(roll_h, rx.at[t], rsend, rrecv, peer(block)) for block in range(1, 8)
-    ]
+    beside_y = (y_hi, z, core, 1 - y_lo, x)
+    RELAY = (
+        ((0, O, 0, 1024), (1, O, 0, 1024), (4, O, 0, 1024)),
+        ((0, XM, 0, 512), (1, XP, 512, 512), (0, F0, 0, 1024), (1, F0, 0, 1024)),
+        ((4, X2, 0, 1024),),
+    )
+
+    def relay(step):
+        copies = []
+        for k, (to, block, first, width) in enumerate(RELAY[step]):
+            py, px = place(block)
+            here = py * 4 + px
+            slot = rx.at[here, :, pl.ds(first, width)]
+            source = roll_h if block == O else slot
+            device = beside_y if to == 4 else to_link[to]
+            copies.append(remote(source, slot, rsend, rrecv.at[3 * step + step // 2 + k], device))
+        return copies
+
+    for copy in relay(0):
+        copy.start()
 
     def part_of(block, row, length):
         if block == O:
@@ -276,7 +292,7 @@
     def project():
         for k in (5, 6, 7, 9):
             local[k].wait()
-        remote(rx.at[pl.ds(0, 7)], rx.at[pl.ds(0, 7)], rsend, rrecv, sibling).wait_recv()
+        relay(2)[0].wait_recv()
         key_sum = jnp.zeros((16, HD), F32)
         value_sum = jnp.zeros((16, HD), F32)
         for k in range(8):
@@ -356,9 +372,12 @@
             hear(known.at[r + 1])
             if r < 2:
                 tell(known.at[r + 2])
+        if r < 2:
+            for copy in relay(r):
+                copy.wait_recv()
+            for copy in relay(r + 1):
+                copy.start()
         if r == 0:
-            for copy in roll_sends:
-                copy.start()
             table()
             for k in (0, 1, 4, 8):
                 local[k].wait()
@@ -412,7 +431,7 @@
 
     for copy in exchange:
         copy.wait_send()
-    remote(rx.at[pl.ds(0, 7)], rx.at[pl.ds(0, 7)], rsend, rrecv, sibling).wait_send()
+    remote(rx.at[pl.ds(0, 7)], rx.at[pl.ds(0, 7)], rsend, grecv, sibling).wait_send()
     remote(wbuf, wbuf, wsend, grecv, sibling).wait_send()
     remote(gbuf, gbuf, gsend, grecv, sibling).wait_send()
     remote(lbuf.at[pl.ds(0, 15)], lbuf.at[pl.ds(0, 15)], lsend, lrecv, sibling).wait_send()
@@ -444,8 +463,8 @@
     attn, whole = pl.pallas_call(
         kernel,
         out_shape=(
-            jax.ShapeDtypeStruct((16, 1024), BF16),
-            jax.ShapeDtypeStruct((8, 128), F32),
+            pltpu.VMEM((16, 1024), BF16),
+            pltpu.VMEM((8, 128), F32),
         ),
         in_specs=[smem, smem] + [anywhere] * 12,
         out_specs=(vmem, vmem),
@@ -479,7 +498,7 @@
             pltpu.VMEM((TENANTS, 512), BF16),
             pltpu.VMEM((128, 128), F32),
             pltpu.VMEM((128, 128), F32),
-            dma((12,)), dma, dma((4, ROUNDS)), dma((2, 7)), dma((4,)), dma((4,)), dma, dma,
+            dma((12,)), dma, dma((4, ROUNDS)), dma((2, 7)), dma((4,)), dma((4,)), dma, dma((8,)),
             dma, dma, dma, dma, dma, dma, pltpu.SemaphoreType.REGULAR((4,)),
         ],
         compiler_params=pltpu.CompilerParams(
@@ -498,7 +517,7 @@
         ),
         in_specs=[vmem, vmem],
         out_specs=(vmem, vmem, vmem),
-    )(attn, whole)
+    )(*(pltpu.with_memory_space_constraint(a, pltpu.VMEM) for a in (attn, whole)))
     return attn_out, gradient, tenant_loss.reshape(TENANTS)
 
 

time: 60.9 us -> 58.3 us (0.957)
  Pallas kernels: 60.1 us -> 57.6 us
    pallas_call x1, Pallas kernels: 58.7 us -> 56.9 us  [local_step(): pl.pallas_call(kernel, out_shape=(pltpu.VMEM((16, 1024), BF16), pltpu.VME...]
    pallas_call x1, Pallas kernels: 1.42 us -> 0.66 us  [local_step(): pl.pallas_call(outputs, out_shape=(jax.ShapeDtypeStruct((16, 1024), BF16)...]
where the time goes in v5:
time: 58.3 us; the launch traced here: 58.2 us
  Pallas kernels  57.6 us (99%)
  between operations  0.64 us (1%)
    pallas_call x1, Pallas kernels, local_step(): pl.pallas_call(kernel, out_shape=(pltpu.VMEM((16, 1024), BF16), pltpu.VME...  56.9 us

profile of v5, /device:TPU:1, one launch (start us, length us, event | category | flops | bytes accessed | tf_op | source)
XLA Modules:
  0.0 58.2 jit_solution(10494250824116301291)
XLA Ops:
  0.6 56.9 %shard_map.157 = (bf16[16,1024]{1,0:T(8,128)(2,1)S(1)}, f32[8,128]{1,0:T(8,128)S(1)}) custom-call(s32[16]{0:T(128)} %clen.1, s32[16]{0:T(128)} %troll.1, bf16[16,1024]{1,0:T(8,128)(2,1)} %roll_h.1, bf16[16,1024]{1,0:T(8,128)(2,1)} %q_h.1, bf16[16,256,128]{2,1,0:T(8,128)(2,1)} %ck_h.1, bf16[16,256,128]{2,1,0:T(8,128)(2,1)} %cv_h.1, bf16[8192,128]{1,0:T(8,128)(2,1)} %wk_h.1, ...), custom_call_target="tpu_custom_call" | custom-call | tf_op jit(solution)/shard_map/pallas_call | solution.py:463
  57.6 0.7 %shard_map.158 = (bf16[16,1024]{1,0:T(8,128)(2,1)}, f32[2,128]{1,0:T(2,128)}, f32[1,64]{1,0:T(1,128)}) custom-call(bf16[16,1024]{1,0:T(8,128)(2,1)S(1)} %get-tuple-element.8.attn, f32[8,128]{1,0:T(8,128)S(1)} %get-tuple-element.9.whole), custom_call_target="tpu_custom_call" | custom-call | tf_op jit(solution)/shard_map/pallas_call | solution.py:511

commit v6 on v5

--- a/solution.py
+++ b/solution.py
@@ -31,10 +31,10 @@
 
 
 LINKS = (
-    quarters(XM, 0, 1, 2, 3) + quarters(X2, 0, 2) + ((F2, 3072, 512), (F2, 3584, 512)),
-    quarters(XP, 0, 1, 2, 3) + quarters(X2, 1, 3) + ((F2, 1024, 512), (F2, 2560, 512)),
-    quarters(F0, 0, 2) + quarters(FM, 0, 1, 2, 3) + ((F2, 0, 512), (F2, 1536, 512)),
-    quarters(F0, 1, 3) + quarters(FP, 0, 1, 2, 3) + ((F2, 512, 512), (F2, 2048, 512)),
+    quarters(XM, 0, 1, 2, 3) + quarters(X2, 0, 2) + ((F2, 2816, 768), (F2, 3840, 256)),
+    quarters(XP, 0, 1, 2, 3) + quarters(X2, 1, 3) + ((F2, 1280, 768), (F2, 3584, 256)),
+    quarters(F0, 0, 2) + quarters(FM, 0, 1, 2, 3) + ((F2, 0, 640), (F2, 2048, 384)),
+    quarters(F0, 1, 3) + quarters(FP, 0, 1, 2, 3) + ((F2, 640, 640), (F2, 2432, 384)),
 )
 ROUNDS = 8
 SENT_AS = (
@@ -51,10 +51,12 @@
     3: (((XM, XP), 2048, 768), ((FM, FP), 640, 640)),
     4: (((X2,), 0, 1280), ((FM, FP), 1280, 768), ((XM, XP), 2816, 1280)),
     5: (((X2,), 1280, 1536), ((FM, FP), 2048, 768), ((FM, FP), 2816, 1280)),
-    6: (((F2,), 0, 1536), ((F2,), 3072, 512), ((X2,), 2816, 1280)),
-    7: (((F2,), 1536, 1536), ((F2,), 3584, 512)),
+    6: (((X2,), 2816, 1280), ((F2,), 0, 2048), ((F2,), 2816, 768)),
+    7: (((F2,), 2048, 768), ((F2,), 3584, 512)),
 }
-FINISH = {3: (O, F0), 4: (XM,), 5: (XP,), 6: (FM, FP, X2), 7: (F2,)}
+FINISH = {3: (O, F0), 4: (XM, XP), 5: (FM, FP), 6: (X2,), 7: (F2,)}
+FAR_PLANE = (10, 2, 6, 8, 9, 11, 14, 1, 3, 4, 5, 7, 12, 13, 15)
+FAR_COLUMN = (8, 9, 7, 6, 10, 5, 11, 4, 12, 3, 13, 2, 14, 1, 15)
 AFTER_Z = ((0, 6), (1, 7))
 
 
@@ -69,9 +71,9 @@
 
 
 def kernel(
-    clen, troll, roll_h, q_h, ck_h, cv_h, wk_h, wv_h, ik_h, iv_h, x_h, up_h, tt_h, adv_h,
+    clen_h, troll_h, roll_h, q_h, ck_h, cv_h, wk_h, wv_h, ik_h, iv_h, x_h, up_h, tt_h, adv_h,
     attn_o, whole_o,
-    wbuf, wv, wk, xh, up, kc, vc, q, rx, ik, iv, tt, adv, tt2, adv2, acc, sbuf, gbuf, lmine, lbuf,
+    clen, troll, wbuf, wv, wk, xh, up, kc, vc, q, rx, ik, iv, tt, adv, tt2, adv2, acc, sbuf, gbuf, lmine, lbuf,
     msg, rbuf, qs, sc, mix, snew, mt, lacc, cnt,
     lsem, wsend, wrecv, zrecv, xsend, xrecv, rsend, rrecv, gsend, grecv,
     lsend, lrecv, msend, mrecv, known,
@@ -134,6 +136,8 @@
                 (q_h, q),
                 (ck_h, kc),
                 (cv_h, vc),
+                (clen_h, clen),
+                (troll_h, troll),
             )
         )
     ]
@@ -290,7 +294,7 @@
         return (pair == row * 8 + h).astype(F32).astype(BF16)
 
     def project():
-        for k in (5, 6, 7, 9):
+        for k in (5, 6, 7, 9, 13):
             local[k].wait()
         relay(2)[0].wait_recv()
         key_sum = jnp.zeros((16, HD), F32)
@@ -320,6 +324,7 @@
 
     def score():
         local[10].wait()
+        local[12].wait()
         place_in_cache = lax.broadcasted_iota(jnp.int32, (8, 256), 1)
         for r in range(16):
             s = lax.dot_general(
@@ -348,12 +353,12 @@
             attn_o[:, h * HD : (h + 1) * HD] = dot(spread(h, True), mixed).astype(BF16)
 
     ones = jnp.ones((8, 128), F32)
-    tile_row = lax.broadcasted_iota(jnp.int32, (8, 128), 0)
+    pair_row = lax.broadcasted_iota(jnp.int32, (2, 128), 0)
 
     def loss_and_count():
         loss_row = exact_dot(ones, lacc[...], ((1,), (1,)))
         count_row = exact_dot(ones, cnt[...], ((1,), (1,)))
-        return jnp.where(tile_row == 2, loss_row, jnp.where(tile_row == 3, count_row, 0.0))
+        return jnp.where(pair_row == 0, loss_row[0:2, :], count_row[0:2, :])
 
     beside = {2: project, 3: score, 4: normalise, 5: mixture}
 
@@ -401,9 +406,11 @@
             lmine[...] = loss_and_count()
 
     group = y * 4 + x
-    mine = lmine[...] + jnp.where(tile_row == 2, exact_dot(ones, lacc[...], ((1,), (1,))), 0.0)
+    mine = lmine[...] + jnp.where(
+        pair_row == 0, exact_dot(ones, lacc[...], ((1,), (1,)))[0:2, :], 0.0
+    )
     lmine[...] = mine
-    for step in range(1, 16):
+    for step in FAR_PLANE:
         remote(lmine, lbuf.at[group], lsend, lrecv, plane_peer(step)[1]).start()
     lbuf[group] = mine
 
@@ -416,10 +423,10 @@
     for k in range(1, 16):
         plane = plane + lbuf[k]
     for k in range(16):
-        msg[k] = plane
         msg[k, 0:2, :] = total[2 * k : 2 * k + 2, :]
+        msg[k, 2:4, :] = plane
     own = z * 2 + core
-    for step in range(1, 16):
+    for step in FAR_COLUMN:
         other, device = column_peer(step)
         remote(msg.at[other], rbuf.at[own], msend, mrecv, device).start()
     rbuf[own] = msg[own]
@@ -456,7 +463,6 @@
     roll_x, queries, cache_k, cache_v, cache_len, tenant_roll, w_key, w_value, ia3_key,
     ia3_value, train_x, upstream, tenant_train, advantage,
 ):
-    smem = pl.BlockSpec(memory_space=pltpu.SMEM)
     vmem = pl.BlockSpec(memory_space=pltpu.VMEM)
     anywhere = pl.BlockSpec(memory_space=pl.ANY)
     dma = pltpu.SemaphoreType.DMA
@@ -464,11 +470,13 @@
         kernel,
         out_shape=(
             pltpu.VMEM((16, 1024), BF16),
-            pltpu.VMEM((8, 128), F32),
+            pltpu.VMEM((4, 128), F32),
         ),
-        in_specs=[smem, smem] + [anywhere] * 12,
+        in_specs=[anywhere] * 14,
         out_specs=(vmem, vmem),
         scratch_shapes=[
+            pltpu.SMEM((16,), jnp.int32),
+            pltpu.SMEM((16,), jnp.int32),
             pltpu.VMEM((7, HALF, HD), BF16),
             pltpu.VMEM((2 * HALF, HD), BF16),
             pltpu.VMEM((2 * HALF, HD), BF16),
@@ -487,10 +495,10 @@
             pltpu.VMEM((8, 512, HD), F32),
             pltpu.VMEM((8, TENANTS, HD), F32),
             pltpu.VMEM((15, 32, HD), F32),
-            pltpu.VMEM((8, 128), F32),
-            pltpu.VMEM((16, 8, 128), F32),
-            pltpu.VMEM((16, 8, 128), F32),
-            pltpu.VMEM((16, 8, 128), F32),
+            pltpu.VMEM((2, 128), F32),
+            pltpu.VMEM((16, 2, 128), F32),
+            pltpu.VMEM((16, 4, 128), F32),
+            pltpu.VMEM((16, 4, 128), F32),
             pltpu.VMEM((128, HD), F32),
             pltpu.VMEM((128, 256), F32),
             pltpu.VMEM((128, HD), F32),
@@ -498,7 +506,7 @@
             pltpu.VMEM((TENANTS, 512), BF16),
             pltpu.VMEM((128, 128), F32),
             pltpu.VMEM((128, 128), F32),
-            dma((12,)), dma, dma((4, ROUNDS)), dma((2, 7)), dma((4,)), dma((4,)), dma, dma((8,)),
+            dma((14,)), dma, dma((4, ROUNDS)), dma((2, 7)), dma((4,)), dma((4,)), dma, dma((8,)),
             dma, dma, dma, dma, dma, dma, pltpu.SemaphoreType.REGULAR((4,)),
         ],
         compiler_params=pltpu.CompilerParams(

time: 58.3 us -> 57.2 us (0.981)
  Pallas kernels: 57.6 us -> 56.4 us
    pallas_call x1, Pallas kernels: 56.9 us -> 55.8 us  [local_step(): pl.pallas_call(kernel, out_shape=(pltpu.VMEM((16, 1024), BF16), pltpu.VME...]
where the time goes in v6:
time: 57.2 us; the launch traced here: 57.1 us
  Pallas kernels  56.4 us (99%)
  between operations  0.64 us (1%)
    pallas_call x1, Pallas kernels, local_step(): pl.pallas_call(kernel, out_shape=(pltpu.VMEM((16, 1024), BF16), pltpu.VME...  55.8 us

profile of v6, /device:TPU:1, one launch (start us, length us, event | category | flops | bytes accessed | tf_op | source)
XLA Modules:
  0.0 57.1 jit_solution(36367670916377266)
XLA Ops:
  0.6 55.8 %shard_map.157 = (bf16[16,1024]{1,0:T(8,128)(2,1)S(1)}, f32[4,128]{1,0:T(4,128)S(1)}) custom-call(s32[16]{0:T(128)} %clen_h.1, s32[16]{0:T(128)} %troll_h.1, bf16[16,1024]{1,0:T(8,128)(2,1)} %roll_h.1, bf16[16,1024]{1,0:T(8,128)(2,1)} %q_h.1, bf16[16,256,128]{2,1,0:T(8,128)(2,1)} %ck_h.1, bf16[16,256,128]{2,1,0:T(8,128)(2,1)} %cv_h.1, ...), custom_call_target="tpu_custom_call" | custom-call | tf_op jit(solution)/shard_map/pallas_call | solution.py:469
  56.4 0.7 %shard_map.158 = (bf16[16,1024]{1,0:T(8,128)(2,1)}, f32[2,128]{1,0:T(2,128)}, f32[1,64]{1,0:T(1,128)}) custom-call(bf16[16,1024]{1,0:T(8,128)(2,1)S(1)} %get-tuple-element.8.attn, f32[4,128]{1,0:T(4,128)S(1)} %get-tuple-element.9.whole), custom_call_target="tpu_custom_call" | custom-call | tf_op jit(solution)/shard_map/pallas_call | solution.py:519

commit v7 on v6

--- a/solution.py
+++ b/solution.py
@@ -368,11 +368,11 @@
     for r in range(ROUNDS):
         for link in range(4):
             link_copy(link, r).wait_recv()
-        if r + 2 < ROUNDS:
-            issue(r + 2)
         for block in Z_SEND.get(r, ()):
             for h in range(2):
                 z_copy(block, h, z_sent).start()
+        if r + 2 < ROUNDS:
+            issue(r + 2)
         if r < 3:
             hear(known.at[r + 1])
             if r < 2:

time: 57.2 us -> 57.2 us (level)
  no operation moved by 1% of the time
where the time goes in v7:
time: 57.2 us; the launch traced here: 57.1 us
  Pallas kernels  56.4 us (99%)
  between operations  0.64 us (1%)
    pallas_call x1, Pallas kernels, local_step(): pl.pallas_call(kernel, out_shape=(pltpu.VMEM((16, 1024), BF16), pltpu.VME...  55.8 us

profile of v7, /device:TPU:1, one launch (start us, length us, event | category | flops | bytes accessed | tf_op | source)
XLA Modules:
  0.0 57.1 jit_solution(14064426470308072459)
XLA Ops:
  0.6 55.8 %shard_map.157 = (bf16[16,1024]{1,0:T(8,128)(2,1)S(1)}, f32[4,128]{1,0:T(4,128)S(1)}) custom-call(s32[16]{0:T(128)} %clen_h.1, s32[16]{0:T(128)} %troll_h.1, bf16[16,1024]{1,0:T(8,128)(2,1)} %roll_h.1, bf16[16,1024]{1,0:T(8,128)(2,1)} %q_h.1, bf16[16,256,128]{2,1,0:T(8,128)(2,1)} %ck_h.1, bf16[16,256,128]{2,1,0:T(8,128)(2,1)} %cv_h.1, ...), custom_call_target="tpu_custom_call" | custom-call | tf_op jit(solution)/shard_map/pallas_call | solution.py:469
  56.4 0.7 %shard_map.158 = (bf16[16,1024]{1,0:T(8,128)(2,1)}, f32[2,128]{1,0:T(2,128)}, f32[1,64]{1,0:T(1,128)}) custom-call(bf16[16,1024]{1,0:T(8,128)(2,1)S(1)} %get-tuple-element.8.attn, f32[4,128]{1,0:T(4,128)S(1)} %get-tuple-element.9.whole), custom_call_target="tpu_custom_call" | custom-call | tf_op jit(solution)/shard_map/pallas_call | solution.py:519
